TPU v7x, 128 devices: a whole 4x4x4 slice. The times are simulated.
128 devices in a mesh: gx: 32 (over x, z, core), gy: 4 (over y).
Axes of the slice: x: 4, y: 4, z: 4, core: 2. Of those that a mesh axis runs over, the one named last changes fastest.
Arguments:
- tracers: float32 [2, 16, 32, 2048], P(None, None, 'gy', 'gx'), may hold values from -6 to 6
- u_face: float32 [16, 32, 2048], P(None, 'gy', 'gx'), may hold values from -0.45 to 0.45
- v_face: float32 [16, 32, 2048], P(None, 'gy', 'gx'), may hold values from -0.45 to 0.45
- thickness: float32 [16, 32, 2048], P(None, 'gy', 'gx'), may hold values from 0.5 to 2
- land_mask: int32 [32, 2048], P('gy', 'gx'), may hold values 0 or 1
- counts: int32 [128, 128], P(('gx', 'gy')), may hold values from 64 to 256, as said below
- ocean_cell: int32 [128, 128, 256], P(('gx', 'gy')), may hold values from 0 to 511
- xgrid_weight: float32 [128, 128, 256], P(('gx', 'gy')), may hold values from 0.05 to 1
- atm_cell: int32 [128, 128, 256], P(('gx', 'gy')), may hold values from 0 to 6911
Outputs:
- tracers_new: float32 [2, 16, 32, 2048], P(None, None, 'gy', 'gx')
- atm_flux: float32 [4, 884736], P(None, ('gx', 'gy'))
Inputs may be any that keep to these rules, and one draw needn't show every extreme that they name: Slots k >= counts[s, o] carry no intersection. One owner, drawn per input, has all 256 slots used from every sender. `ocean_cell`: indexes the sender's tile row-major over 8 x 64 cells; read only in used slots. `atm_cell`: indexes the owner's 6912 cells; slot (s, o, k) here belongs to slot (s, o, k) of ocean_cell.
All inputs are finite; a program needn't handle non-finite values. No bound on the sum of `land_mask` on one device may be relied on, other than what follows from the above.
Results may differ from a plain program's by a relative error of at most 0.0003.
Values sent between devices are 32-bit elements; how exact they have to be, the bound alone decides.
No kernel may reach another device: no remote copies, remote signals or barrier semaphores. Data moves between devices by JAX's collectives and lax.ppermute only.
A program may use at most 64 MiB of HBM per device.

v0:
```python
import jax
import jax.numpy as jnp
from jax import lax
from jax.sharding import PartitionSpec as P

A_DEV = 6912


def extended(array, sides, width):
    for axis, dim in sides:
        size, length = (lax.axis_size(axis), array.shape[dim])
        up = [(i, (i + 1) % size) for i in range(size - 1)]
        down = [(j, i) for i, j in up]
        last = lax.slice_in_dim(array, length - width, length, axis=dim)
        first = lax.slice_in_dim(array, 0, width, axis=dim)
        before = lax.ppermute(last, axis, up)
        after = lax.ppermute(first, axis, down)
        array = jnp.concatenate([before, array, after], axis=dim)
    return array


def window_cut(values, lead_cut, tail_cut, sweep_axis):
    return lax.slice_in_dim(values, lead_cut, values.shape[sweep_axis] - tail_cut, axis=sweep_axis)


def ppm_sweep(padded, velocity, wet_cells, sweep_axis):
    edge_values = (
        7.0 * (window_cut(padded, 1, 2, sweep_axis) + window_cut(padded, 2, 1, sweep_axis))
        - (window_cut(padded, 0, 3, sweep_axis) + window_cut(padded, 3, 0, sweep_axis))
    ) / 12.0
    left_edge = window_cut(edge_values, 0, 1, sweep_axis)
    right_edge = window_cut(edge_values, 1, 0, sweep_axis)
    centre_vals = window_cut(padded, 2, 2, sweep_axis)
    slope_diff = right_edge - left_edge
    curvature = 6.0 * centre_vals - 3.0 * (left_edge + right_edge)
    courant = (
        window_cut(velocity, 2, 3, sweep_axis)
        * window_cut(wet_cells, 2, 3, sweep_axis)
        * window_cut(wet_cells, 3, 2, sweep_axis)
    )
    backward = -courant
    up_flux = courant * (
        window_cut(right_edge, 0, 1, sweep_axis)
        - 0.5
        * courant
        * (
            window_cut(slope_diff, 0, 1, sweep_axis)
            - (1.0 - courant * (2.0 / 3.0)) * window_cut(curvature, 0, 1, sweep_axis)
        )
    )
    down_flux = courant * (
        window_cut(left_edge, 1, 0, sweep_axis)
        + 0.5
        * backward
        * (
            window_cut(slope_diff, 1, 0, sweep_axis)
            + (1.0 - backward * (2.0 / 3.0)) * window_cut(curvature, 1, 0, sweep_axis)
        )
    )
    flux_face = jnp.where(courant >= 0.0, up_flux, down_flux)
    return window_cut(padded, 3, 3, sweep_axis) - (
        window_cut(flux_face, 1, 0, sweep_axis) - window_cut(flux_face, 0, 1, sweep_axis)
    )


def vertical_remap(fields, thickness):
    levels = thickness.shape[0]
    bottoms = jnp.cumsum(thickness, axis=0)
    starts = jnp.concatenate([jnp.zeros_like(bottoms[:1]), bottoms[:-1]], axis=0)
    target_thick = bottoms[-1] / levels
    results = []
    for target_level in range(levels):
        layer_top = target_thick * target_level
        layer_base = target_thick * (target_level + 1)
        shared_depth = jnp.maximum(
            jnp.minimum(bottoms, layer_base) - jnp.maximum(starts, layer_top), 0.0
        )
        results.append(jnp.sum(shared_depth[None] * fields, axis=1) / target_thick)
    return jnp.stack(results, axis=1)


def surface_fields(tracers, u_face, v_face):
    east_current = u_face[0]
    north_current = v_face[0]
    surface_speed = jnp.sqrt(east_current * east_current + north_current * north_current + 0.01)
    return jnp.stack(
        [
            tracers[0, 0] * surface_speed,
            tracers[1, 0] * surface_speed,
            east_current * surface_speed,
            north_current * surface_speed,
        ]
    ).reshape(4, -1)


def on_device(
    tracers, u_face, v_face, thickness, land_mask, counts, ocean_cell, xgrid_weight, atm_cell
):
    levels = tracers.shape[1]
    tile_rows = tracers.shape[2]
    tile_cols = tracers.shape[3]
    wet_cells = land_mask.astype(jnp.float32)
    fields = surface_fields(tracers, u_face, v_face)
    owners = counts.shape[1]
    slot_count = ocean_cell.shape[2]
    cell_index = ocean_cell.reshape(owners * slot_count)
    slot_ids = lax.broadcasted_iota(jnp.int32, (owners, slot_count), 1)
    slot_used = (slot_ids < counts[0][:, None]).astype(jnp.float32).reshape(-1)
    row_share = xgrid_weight.reshape(-1) * wet_cells.reshape(-1)[cell_index] * slot_used
    picked = fields[:, cell_index] * row_share[None]
    payload = jnp.concatenate([picked, row_share[None]], axis=0).reshape(5, owners, slot_count)
    received = lax.all_to_all(payload, ("gx", "gy"), split_axis=1, concat_axis=1, tiled=True)
    targets = atm_cell.reshape(-1)
    totals = jnp.zeros((5, A_DEV), jnp.float32).at[:, targets].add(received.reshape(5, -1))
    atm_flux = totals[:4] / jnp.maximum(totals[4:5], 0.2)
    stacked = jnp.concatenate(
        [tracers.reshape(2 * levels, tile_rows, tile_cols), u_face, v_face, wet_cells[None]], axis=0
    )
    widened = extended(stacked, (("gy", 1),), 3)
    padded = extended(widened, (("gx", 2),), 3)
    field_pad = padded[: 2 * levels].reshape(2, levels, tile_rows + 6, tile_cols + 6)
    east_pad = padded[2 * levels : 3 * levels][None]
    north_pad = padded[3 * levels : 4 * levels][None]
    wet_pad = padded[4 * levels :][None]
    x_swept = ppm_sweep(field_pad, east_pad, wet_pad, 3)
    advected = ppm_sweep(x_swept, north_pad[..., 3:-3], wet_pad[..., 3:-3], 2)
    tracers_new = vertical_remap(advected, thickness)
    return (tracers_new, atm_flux)


def solution(mesh):
    placed = (
        P(None, None, "gy", "gx"),
        P(None, "gy", "gx"),
        P(None, "gy", "gx"),
        P(None, "gy", "gx"),
        P("gy", "gx"),
        P(("gx", "gy"), None),
        P(("gx", "gy"), None, None),
        P(("gx", "gy"), None, None),
        P(("gx", "gy"), None, None),
    )
    return jax.shard_map(
        on_device,
        mesh=mesh,
        in_specs=placed,
        out_specs=(P(None, None, "gy", "gx"), P(None, ("gx", "gy"))),
        check_vma=False,
    )
```

profile of v0, /device:TPU:1, one launch (start us, length us, event | category | flops | bytes accessed | tf_op | source)
XLA Modules:
  0.0 562.1 jit_solution(8114539273220438389)
XLA Ops:
  0.6 0.7 fusion.40
  1.4 1.0 pad_maximum_fusion.3
  2.4 4.0 collective-permute-start
  6.5 1.3 collective-permute-start.1
  7.8 0.7 bitcast_multiply_fusion.2
  8.6 1.0 copy.125
  9.9 203.3 %gather_fusion.1 = f32[32768]{0:T(1024)S(1)} fusion(f32[512]{0:T(512)S(1)} %reshape.292, s32[32768]{0:T(1024)S(1)} %broadcast_clamp_fusion), kind=kCustom, calls=%fused_computation.1 | custom fusion | bytes 393216 | tf_op jit(solution)/shard_map/gather | solution.py:109
  214.0 108.2 %gather_fusion = f32[32768,4]{1,0:T(8,128)} fusion(f32[4,512]{0,1:T(8,128)S(1)} %copy.114, s32[32768]{0:T(1024)S(1)} %broadcast_clamp_fusion), kind=kCustom, calls=%fused_computation | custom fusion | bytes 1179648 | tf_op jit(solution)/shard_map/gather | solution.py:110
  322.2 10.0 %copy.115 = f32[4,128,256]{2,1,0:T(8,128)S(1)} copy(f32[4,128,256]{0,2,1:T(8,128)} %bitcast.130) | data formatting | bytes 1048576 | tf_op jit(solution)/shard_map/gather | solution.py:110
  332.3 1.4 copy.116
  333.7 12.0 %all-to-all-start = ((f32[5,128,256]{2,0,1:T(8,128)}), f32[5,128,256]{2,0,1:T(8,128)S(1)}, u32[]{:S(2)}, u32[]{:S(2)}) async-start(f32[5,128,256]{2,0,1:T(8,128)} %copy.116), calls=%async_computation | async-start | bytes 2097152 | tf_op jit(solution)/shard_map/all_to_all | solution.py:112
  345.7 0.7 fusion.41
  346.6 0.8 compare_select_fusion.1
  348.4 3.0 collective-permute-start.3
  351.3 2.6 collective-permute-start.2
  356.2 0.6 copy.112
  356.8 0.6 copy.113
  362.3 0.7 copy.118
  363.0 2.7 all-to-all-done
  365.7 9.0 %copy.117 = f32[32768,5]{1,0:T(8,128)} copy(f32[32768,5]{0,1:T(8,128)S(1)} %bitcast.134) | data formatting | bytes 1310720 | tf_op jit(solution)/shard_map/reshape | solution.py:114
  374.6 176.1 %scatter_custom_fusion = f32[5,6912]{0,1:T(8,128)} fusion(s32[32768]{0:T(1024)} %bitcast.143, f32[32768,5]{1,0:T(8,128)} %copy.117, f32[]{:T(128)} %constant.27.clone.1), kind=kCustom, calls=%fused_computation.6 | custom fusion | flops 163840 | bytes 138752 | tf_op jit(solution)/shard_map/scatter-add | solution.py:114
  550.8 4.1 fusion
  554.9 4.1 slice_divide_fusion
  559.0 3.2 copy.119
  (122 shorter events, 8.9 us)
Async XLA Ops:
  0.6 345.1 %copy-start = (f32[16,8,64]{2,1,0:T(8,128)S(1)}, f32[16,8,64]{2,1,0:T(8,128)}, u32[]{:S(2)}) copy-start(f32[16,8,64]{2,1,0:T(8,128)} %param.12) | copy-start | bytes 98308
  2.4 345.0 %collective-permute-start = (f32[65,3,64]{2,1,0:T(4,128)S(1)}, f32[65,3,64]{2,1,0:T(4,128)S(1)}, u32[]{:S(2)}, u32[]{:S(2)}) collective-permute-start(f32[65,3,64]{2,1,0:T(4,128)S(1)} %get-tuple-element.34), channel_id=1, source_target_pairs={{0,1},{1,2},{2,3},{4,5},{5,6},{6,7},{8,9},{9,10},{10,11},{12,13},{... | collective-permute-start | bytes 149768 | tf_op jit(solution)/shard_map/ppermute | solution.py:16
  6.5 341.0 %collective-permute-start.1 = (f32[65,3,64]{2,1,0:T(4,128)S(1)}, f32[65,3,64]{2,1,0:T(4,128)S(1)}, u32[]{:S(2)}, u32[]{:S(2)}) collective-permute-start(f32[65,3,64]{2,1,0:T(4,128)S(1)} %get-tuple-element.35), channel_id=1, source_target_pairs={{1,0},{2,1},{3,2},{5,4},{6,5},{7,6},{9,8},{10,9},{11,10},{13,12},{... | collective-permute-start | bytes 149768 | tf_op jit(solution)/shard_map/ppermute | solution.py:17
  9.8 203.6 %copy-start.2 = (f32[2,16,8,64]{3,2,1,0:T(8,128)S(1)}, f32[2,16,8,64]{3,2,1,0:T(8,128)}, u32[]{:S(2)}) copy-start(f32[2,16,8,64]{3,2,1,0:T(8,128)} %param.9) | copy-start | bytes 196612
  9.8 203.5 %copy-start.3 = (f32[16,8,64]{2,1,0:T(8,128)S(1)}, f32[16,8,64]{2,1,0:T(8,128)}, u32[]{:S(2)}) copy-start(f32[16,8,64]{2,1,0:T(8,128)} %param.11) | copy-start | bytes 98308
  9.8 203.5 %copy-start.4 = (f32[16,8,64]{2,1,0:T(8,128)S(1)}, f32[16,8,64]{2,1,0:T(8,128)}, u32[]{:S(2)}) copy-start(f32[16,8,64]{2,1,0:T(8,128)} %param.10) | copy-start | bytes 98308
  9.8 203.8 %copy-start.5 = (f32[1,128,256]{2,1,0:T(8,128)S(1)}, f32[1,128,256]{2,1,0:T(8,128)}, u32[]{:S(2)}) copy-start(f32[1,128,256]{2,1,0:T(8,128)} %param.16) | copy-start | bytes 393220
  9.8 203.8 %copy-start.12 = (s32[1,128]{1,0:T(1,128)S(1)}, s32[1,128]{1,0:T(1,128)}, u32[]{:S(2)}) copy-start(s32[1,128]{1,0:T(1,128)} %param.14) | copy-start | bytes 1540
  332.2 14.3 %copy-start.11 = (s32[1,128,256]{2,1,0:T(8,128)S(1)}, s32[1,128,256]{2,1,0:T(8,128)}, u32[]{:S(2)}) copy-start(s32[1,128,256]{2,1,0:T(8,128)} %param.17) | copy-start | bytes 393220
  333.7 32.0 %all-to-all-start = ((f32[5,128,256]{2,0,1:T(8,128)}), f32[5,128,256]{2,0,1:T(8,128)S(1)}, u32[]{:S(2)}, u32[]{:S(2)}) async-start(f32[5,128,256]{2,0,1:T(8,128)} %copy.116), calls=%async_computation | async-start | bytes 2097152 | tf_op jit(solution)/shard_map/all_to_all | solution.py:112
  348.4 9.7 %collective-permute-start.3 = (f32[65,14,3]{0,1,2:T(8,128)S(1)}, f32[65,14,3]{0,1,2:T(8,128)S(1)}, u32[]{:S(2)}, u32[]{:S(2)}) collective-permute-start(f32[65,14,3]{0,1,2:T(8,128)S(1)} %copy.83), channel_id=1, source_target_pairs={{4,0},{8,4},{12,8},{16,12},{20,16},{24,20},{28,24},{32,28},{36,32}... | collective-permute-start | bytes 32768 | tf_op jit(solution)/shard_map/ppermute | solution.py:17
  351.3 6.1 %collective-permute-start.2 = (f32[65,14,3]{0,1,2:T(8,128)S(1)}, f32[65,14,3]{0,1,2:T(8,128)S(1)}, u32[]{:S(2)}, u32[]{:S(2)}) collective-permute-start(f32[65,14,3]{0,1,2:T(8,128)S(1)} %copy.82), channel_id=1, source_target_pairs={{0,4},{4,8},{8,12},{12,16},{16,20},{20,24},{24,28},{28,32},{32,36}... | collective-permute-start | bytes 32768 | tf_op jit(solution)/shard_map/ppermute | solution.py:16
  360.4 0.9 copy-start.6
  360.4 0.9 copy-start.7
  360.4 0.9 copy-start.8
  360.4 0.9 copy-start.9
  360.4 0.9 copy-start.10
  550.8 4.1 copy-start.1
where the time goes:
time: 564 us; the launch traced here: 562 us
  local copies, waits for them, and re-layouts  343 us (61%)
  other arithmetic  192 us (34%)
  starting transfers between devices  22.9 us (4%)
    gather x3, local copies, waits for them, and re-layouts, on_device(): wet_cells.reshape(-1)[cell_index]  203 us
    scatter-add x1, other arithmetic, on_device(): jnp.zeros((5, A_DEV), jnp.float32).at[:, targets]  176 us
    gather x2, local copies, waits for them, and re-layouts, on_device(): picked = fields[:, cell_index] * row_share[None]  118 us
    all_to_all x1, starting transfers between devices, on_device(): lax.all_to_all(payload, ('gx', 'gy'), split_axis=1, concat_axis=1, tiled=...  12 us
  transfers between devices with their start and end apart: 5, of which 2 were waited for; matrix products, arithmetic and copies ran while one was open for 60% of the time, Pallas kernels for 0%

commit v1 on v0

--- a/solution.py
+++ b/solution.py
@@ -1,9 +1,104 @@
 import jax
 import jax.numpy as jnp
 from jax import lax
+from jax.experimental import pallas as pl
+from jax.experimental.pallas import tpu as pltpu
 from jax.sharding import PartitionSpec as P
 
 A_DEV = 6912
+def lane_take(table, lanes):
+    return jnp.take_along_axis(table, lanes, axis=1, mode="promise_in_bounds")
+
+def gather_kernel(tracers, u_face, v_face, land_mask, counts, ocean_cell, weight, payload):
+    def packed(x):
+        return jnp.concatenate([x[0:4, :], x[4:8, :]], axis=1)
+    wet = packed(land_mask[...].astype(jnp.float32))
+    east = packed(u_face[0]); north = packed(v_face[0])
+    speed = jnp.sqrt(east * east + north * north + 0.01) * wet
+    fields = [packed(tracers[0, 0]) * speed, packed(tracers[1, 0]) * speed, east * speed, north * speed, wet]
+    tables = [[jnp.broadcast_to(f[q:q+1, :], (8, 128)) for q in range(4)] for f in fields]
+    used = jnp.broadcast_to(counts[...], (8, 128))
+    sub = lax.broadcasted_iota(jnp.int32, (8, 128), 0)
+    lane_ids = lax.broadcasted_iota(jnp.int32, (8, 128), 1)
+    def step(g, _):
+        o = pl.multiple_of(g * 8, 8)
+        count = lane_take(used, sub + o)
+        for h in range(2):
+            cell = ocean_cell[0, pl.ds(o, 8), h*128:(h+1)*128]
+            share = jnp.where(lane_ids + h*128 < count, weight[0, pl.ds(o, 8), h*128:(h+1)*128], 0.0)
+            lanes = (cell & 63) | ((cell >> 2) & 64)
+            odd = (cell & 64) != 0
+            upper = (cell & 128) != 0
+            for f in range(5):
+                a, b, c, d = [lane_take(t, lanes) for t in tables[f]]
+                val = jnp.where(upper, jnp.where(odd, d, c), jnp.where(odd, b, a))
+                payload[pl.ds(g * 80 + f*2+h, 8, stride=10), :] = val * share
+        return 0
+    lax.fori_loop(0, 16, step, 0, unroll=2)
+
+def gather(tracers, u_face, v_face, land_mask, counts, ocean_cell, weight):
+    return pl.pallas_call(gather_kernel, grid=(1,),
+      in_specs=[pl.BlockSpec((2,1,8,64), lambda i:(0,0,0,0)), pl.BlockSpec((1,8,64), lambda i:(0,0,0)), pl.BlockSpec((1,8,64), lambda i:(0,0,0)),
+        pl.BlockSpec((8,64), lambda i:(0,0)), pl.BlockSpec((1,128), lambda i:(0,0)), pl.BlockSpec((1,128,256), lambda i:(0,0,0)), pl.BlockSpec((1,128,256), lambda i:(0,0,0))],
+      out_specs=pl.BlockSpec((1280,128), lambda i:(0,0)),
+      out_shape=jax.ShapeDtypeStruct((1280,128), jnp.float32),
+      name="gather_rows")(tracers, u_face, v_face, land_mask, counts, ocean_cell, weight)
+
+def scatter_kernel(received, atm_cell, flux, rows_a, rows_b, acc, fin):
+    iota16 = lax.broadcasted_iota(jnp.int32, (16, 128), 0).astype(jnp.bfloat16)
+    zero = jnp.zeros((16,128), jnp.bfloat16); one = jnp.ones((16,128), jnp.bfloat16)
+    def bc(row):
+        return jnp.broadcast_to(row, (16, 128)).astype(jnp.bfloat16)
+    def build(g, slot):
+        s0 = pl.multiple_of(g * 8, 8)
+        for h in range(2):
+            cell = atm_cell[0, pl.ds(s0, 8), h*128:(h+1)*128]
+            high = (cell >> 8).astype(jnp.float32)
+            low = (cell & 255).astype(jnp.float32)
+            pieces = []
+            for f in range(5):
+                val = received[pl.ds(g * 80 + f*2+h, 8, stride=10), :]
+                top = val.astype(jnp.bfloat16).astype(jnp.float32)
+                pieces += [top, val - top]
+            for s in range(8):
+                cols = slice((s*2+h)*128, (s*2+h+1)*128)
+                lo = bc(low[s:s+1, :])
+                for k in range(16):
+                    rows_b[slot, k*16:(k+1)*16, cols] = jnp.where(lo == iota16 + jnp.bfloat16(k*16), one, zero)
+                hi = bc(high[s:s+1, :])
+                m = [hi == iota16, hi == iota16 + jnp.bfloat16(16)]
+                for j in range(10):
+                    p = bc(pieces[j][s:s+1, :])
+                    for k in range(2):
+                        rows_a[slot, (j*2+k)*16:(j*2+k+1)*16, cols] = jnp.where(m[k], p, zero)
+    def mult(slot):
+        acc[...] += lax.dot_general(rows_a[slot], rows_b[slot], (((1,),(1,)),((),())), preferred_element_type=jnp.float32)
+    acc[...] = jnp.zeros_like(acc)
+    build(0, 0)
+    def step(i, _):
+        build(2*i+1, 1)
+        mult(0)
+        build(jnp.minimum(2*i+2, 15), 0)
+        mult(1)
+        return 0
+    lax.fori_loop(0, 8, step, 0)
+    for half in range(2):
+        for f in range(5):
+            fin[half*160+f*32:half*160+f*32+32, :] = acc[f*64:f*64+32, half*128:half*128+128] + acc[f*64+32:f*64+64, half*128:half*128+128]
+    for hi in range(27):
+        for half in range(2):
+            num = fin[pl.ds(half*160+hi, 4, stride=32), :]
+            den = fin[half*160+128+hi:half*160+129+hi, :]
+            flux[:, hi*256+half*128:hi*256+half*128+128] = num / jnp.maximum(den, 0.2)
+
+def scatter(received, atm_cell):
+    return pl.pallas_call(scatter_kernel,
+      in_specs=[pl.BlockSpec(memory_space=pltpu.VMEM)]*2,
+      out_specs=pl.BlockSpec(memory_space=pltpu.VMEM),
+      out_shape=jax.ShapeDtypeStruct((4,A_DEV), jnp.float32),
+      scratch_shapes=[pltpu.VMEM((2,320,2048), jnp.bfloat16), pltpu.VMEM((2,256,2048), jnp.bfloat16), pltpu.VMEM((320,256), jnp.float32), pltpu.VMEM((320,128), jnp.float32)],
+      compiler_params=pltpu.CompilerParams(vmem_limit_bytes=40*2**20),
+      name="scatter_add")(received, atm_cell)
 
 
 def extended(array, sides, width):
@@ -79,20 +174,6 @@
     return jnp.stack(results, axis=1)
 
 
-def surface_fields(tracers, u_face, v_face):
-    east_current = u_face[0]
-    north_current = v_face[0]
-    surface_speed = jnp.sqrt(east_current * east_current + north_current * north_current + 0.01)
-    return jnp.stack(
-        [
-            tracers[0, 0] * surface_speed,
-            tracers[1, 0] * surface_speed,
-            east_current * surface_speed,
-            north_current * surface_speed,
-        ]
-    ).reshape(4, -1)
-
-
 def on_device(
     tracers, u_face, v_face, thickness, land_mask, counts, ocean_cell, xgrid_weight, atm_cell
 ):
@@ -100,19 +181,9 @@
     tile_rows = tracers.shape[2]
     tile_cols = tracers.shape[3]
     wet_cells = land_mask.astype(jnp.float32)
-    fields = surface_fields(tracers, u_face, v_face)
-    owners = counts.shape[1]
-    slot_count = ocean_cell.shape[2]
-    cell_index = ocean_cell.reshape(owners * slot_count)
-    slot_ids = lax.broadcasted_iota(jnp.int32, (owners, slot_count), 1)
-    slot_used = (slot_ids < counts[0][:, None]).astype(jnp.float32).reshape(-1)
-    row_share = xgrid_weight.reshape(-1) * wet_cells.reshape(-1)[cell_index] * slot_used
-    picked = fields[:, cell_index] * row_share[None]
-    payload = jnp.concatenate([picked, row_share[None]], axis=0).reshape(5, owners, slot_count)
-    received = lax.all_to_all(payload, ("gx", "gy"), split_axis=1, concat_axis=1, tiled=True)
-    targets = atm_cell.reshape(-1)
-    totals = jnp.zeros((5, A_DEV), jnp.float32).at[:, targets].add(received.reshape(5, -1))
-    atm_flux = totals[:4] / jnp.maximum(totals[4:5], 0.2)
+    payload = gather(tracers, u_face, v_face, land_mask, counts, ocean_cell, xgrid_weight)
+    received = lax.all_to_all(payload.reshape(128, 1, 1280), ("gx", "gy"), split_axis=0, concat_axis=0, tiled=True)
+    atm_flux = scatter(received.reshape(1280, 128), atm_cell)
     stacked = jnp.concatenate(
         [tracers.reshape(2 * levels, tile_rows, tile_cols), u_face, v_face, wet_cells[None]], axis=0
     )

time: 564 us -> 53.6 us (0.10)
  local copies, waits for them, and re-layouts: 343 us -> 5.05 us
  other arithmetic: 192 us -> 5.57 us
  Pallas kernels: 0 us -> 15.4 us
    gather x5 -> x0, local copies, waits for them, and re-layouts: 322 us -> none  [the longest x3 203 us: on_device(): wet_cells.reshape(-1)[cell_index]]
    scatter-add x1 -> x0, other arithmetic: 176 us -> none  [on_device(): jnp.zeros((5, A_DEV), jnp.float32).at[:, targets]]
    pallas_call x0 -> x2, Pallas kernels: none -> 15.4 us  [the longest x1 12 us: scatter(): pl.pallas_call(scatter_kernel, in_specs=[pl.BlockSpec(memory_space=pltpu....]
    reshape x2 -> x0, local copies, waits for them, and re-layouts: 9.05 us -> none  [the longest x1 8.98 us: on_device(): received.reshape(5, -1)]
  transfers between devices with their start and end apart: 5 -> 5, of which waited for: 2 -> 1; matrix products, arithmetic and copies ran while one was open for 60% -> 13% of each run, Pallas kernels for 0% -> 6%
where the time goes in v1:
time: 53.6 us; the launch traced here: 53.2 us
  starting transfers between devices  22.9 us (43%)
  Pallas kernels  15.4 us (29%)
  other arithmetic  5.57 us (10%)
  local copies, waits for them, and re-layouts  5.05 us (9%)
  waiting for transfers between devices  3 us (6%)
  between operations  1.23 us (2%)
    pallas_call x1, Pallas kernels, scatter(): pl.pallas_call(scatter_kernel, in_specs=[pl.BlockSpec(memory_space=pltpu....  12 us
    all_to_all x1, starting transfers between devices, on_device(): lax.all_to_all(payload.reshape(128, 1, 1280), ('gx', 'gy'), split_axis=0,...  12 us
    ppermute x2, starting transfers between devices, extended(): before = lax.ppermute(last, axis, up)  7.69 us
    pallas_call x1, Pallas kernels, gather(): pl.pallas_call(gather_kernel, grid=(1,), in_specs=[pl.BlockSpec((2, 1, 8,...  3.38 us
    ppermute x2, starting transfers between devices, extended(): after = lax.ppermute(first, axis, down)  3.2 us
    ppermute x2, waiting for transfers between devices, extended(): after = lax.ppermute(first, axis, down)  2.99 us
    unnamed x15, local copies, waits for them, and re-layouts  1.82 us
  transfers between devices with their start and end apart: 5, of which 1 were waited for; matrix products, arithmetic and copies ran while one was open for 13% of the time, Pallas kernels for 6%

profile of v1, /device:TPU:1, one launch (start us, length us, event | category | flops | bytes accessed | tf_op | source)
XLA Modules:
  0.0 53.2 jit_solution(14291077780526987687)
XLA Ops:
  0.6 0.7 %convert_bitcast_fusion = f32[1,8,64]{2,1,0:T(8,128)S(1)} fusion(s32[8,64]{1,0:T(8,128)} %land_mask.1), kind=kLoop, calls=%fused_computation.127 | loop fusion | flops 512 | bytes 4096 | tf_op jit(solution)/shard_map/broadcast_in_dim | solution.py:188
  1.4 1.0 %pad_maximum_fusion.2 = f32[65,8,64]{2,1,0:T(8,128)S(1)} fusion(f32[1,8,64]{2,1,0:T(8,128)S(1)} %convert_bitcast_fusion, f32[16,8,64]{2,1,0:T(8,128)} %v_face.1, f32[16,8,64]{2,1,0:T(8,128)} %u_face.1, f32[32,8,64]{2,1,0:T(8,128)} %bitcast.114), kind=kLoop, calls=%fused_computation.2 | loop fusion | flops 99840 | bytes 266240 | tf_op jit(solution)/shard_map/concatenate | solution.py:187
  2.4 4.0 %collective-permute-start = (f32[65,3,64]{2,1,0:T(4,128)S(1)}, f32[65,3,64]{2,1,0:T(4,128)S(1)}, u32[]{:S(2)}, u32[]{:S(2)}) collective-permute-start(f32[65,3,64]{2,1,0:T(4,128)S(1)} %get-tuple-element.24), channel_id=1, source_target_pairs={{0,1},{1,2},{2,3},{4,5},{5,6},{6,7},{8,9},{9,10},{10,11},{12,13},{... | collective-permute-start | bytes 149768 | tf_op jit(solution)/shard_map/ppermute | solution.py:111
  6.5 1.3 %collective-permute-start.1 = (f32[65,3,64]{2,1,0:T(4,128)S(1)}, f32[65,3,64]{2,1,0:T(4,128)S(1)}, u32[]{:S(2)}, u32[]{:S(2)}) collective-permute-start(f32[65,3,64]{2,1,0:T(4,128)S(1)} %get-tuple-element.25), channel_id=1, source_target_pairs={{1,0},{2,1},{3,2},{5,4},{6,5},{7,6},{9,8},{10,9},{11,10},{13,12},{... | collective-permute-start | bytes 149768 | tf_op jit(solution)/shard_map/ppermute | solution.py:112
  7.8 3.4 %gather_rows.1 = f32[1280,128]{1,0:T(8,128)} custom-call(f32[2,16,8,64]{3,2,1,0:T(8,128)} %tracers.1, f32[16,8,64]{2,1,0:T(8,128)} %u_face.1, f32[16,8,64]{2,1,0:T(8,128)} %v_face.1, s32[8,64]{1,0:T(8,128)} %land_mask.1, s32[1,128]{1,0:T(1,128)} %counts.1, s32[1,128,256]{2,1,0:T(8,128)} %ocean_cell.1, f32[1,128,256]{2,1,0:T(8,128)} %weight.1), custom_call_target="tpu_custom_call" | custom-call | tf_op jit(solution)/shard_map/gather_rows/pallas_call | solution.py:40
  11.1 12.0 %all-to-all-start = ((f32[128,1,1280]{2,1,0:T(1,128)}), f32[128,1,1280]{2,1,0:T(1,128)S(1)}, u32[]{:S(2)}, u32[]{:S(2)}) async-start(f32[128,1,1280]{2,1,0:T(1,128)} %bitcast.113), calls=%async_computation | async-start | bytes 1310720 | tf_op jit(solution)/shard_map/all_to_all | solution.py:185
  23.2 0.7 %fusion.36 = f32[16,8,64]{2,1,0:T(8,128)S(1)} fusion(f32[16,8,64]{2,1,0:T(8,128)S(1)} %copy-done), kind=kOutput, calls=%fused_computation.137 | output fusion | flops 122880 | bytes 65536 | tf_op jit(solution)/shard_map/jit(cumsum)/reduce_window_sum | solution.py:163
  24.0 0.8 %copy-done.3 = f32[2,16,8,64]{3,2,1,0:T(8,128)S(1)} copy-done((f32[2,16,8,64]{3,2,1,0:T(8,128)S(1)}, f32[2,16,8,64]{3,2,1,0:T(8,128)}, u32[]{:S(2)}) %copy-start.3) | copy-done | bytes 65560
  24.9 0.2 fusion.32
  25.1 0.3 copy.67
  25.4 3.7 %collective-permute-start.2 = (f32[65,14,3]{0,1,2:T(8,128)S(1)}, f32[65,14,3]{0,1,2:T(8,128)S(1)}, u32[]{:S(2)}, u32[]{:S(2)}) collective-permute-start(f32[65,14,3]{0,1,2:T(8,128)S(1)} %copy.67), channel_id=1, source_target_pairs={{0,4},{4,8},{8,12},{12,16},{16,20},{20,24},{24,28},{28,32},{32,36}... | collective-permute-start | bytes 32768 | tf_op jit(solution)/shard_map/ppermute | solution.py:111
  29.1 0.3 copy.68
  29.4 1.9 %collective-permute-start.3 = (f32[65,14,3]{0,1,2:T(8,128)S(1)}, f32[65,14,3]{0,1,2:T(8,128)S(1)}, u32[]{:S(2)}, u32[]{:S(2)}) collective-permute-start(f32[65,14,3]{0,1,2:T(8,128)S(1)} %copy.68), channel_id=1, source_target_pairs={{4,0},{8,4},{12,8},{16,12},{20,16},{24,20},{28,24},{32,28},{36,32}... | collective-permute-start | bytes 32768 | tf_op jit(solution)/shard_map/ppermute | solution.py:112
  31.8 0.3 copy.69
  32.1 3.0 %collective-permute-done.3 = f32[65,14,3]{0,1,2:T(8,128)S(1)} collective-permute-done((f32[65,14,3]{0,1,2:T(8,128)S(1)}, f32[65,14,3]{0,1,2:T(8,128)S(1)}, u32[]{:S(2)}, u32[]{:S(2)}) %collective-permute-start.3) | collective-permute-done | bytes 10952 | tf_op jit(solution)/shard_map/ppermute | solution.py:112
  35.1 0.3 copy.70
  35.4 0.5 pad_maximum_fusion.1
  37.2 0.8 %slice-done = f32[32,14,70]{2,1,0:T(8,128)S(1)} async-done(((f32[65,14,70]{2,1,0:T(8,128)}), f32[32,14,70]{2,1,0:T(8,128)S(1)}, s32[]{:S(2)}) %slice-start) | async-done | bytes 125464 | tf_op jit(solution)/shard_map/slice | solution.py:192
  38.1 0.2 fusion.12
  38.6 0.3 fusion.5
  39.2 0.6 %multiply_reduce_fusion = (f32[2,8,64]{2,0,1:T(2,128)S(1)}, f32[2,8,64]{2,0,1:T(2,128)S(1)}, f32[2,8,64]{2,0,1:T(2,128)S(1)}, f32[2,8,64]{2,0,1:T(2,128)S(1)}, f...) fusion(f32[16,8,64]{2,0,1:T(8,128)S(1)} %copy.98, ...), kind=kLoop, calls=%fused_computation.51 | loop fusion | flops 540672 | bytes 786432 | tf_op jit(solution)/shard_map/reduce_sum | solution.py:173
  40.2 0.7 %copy.100 = f32[2,16,8,64]{3,2,1,0:T(8,128)} copy(f32[2,16,8,64]{3,0,2,1:T(2,128)S(1)} %constant_dynamic-update-slice_fusion) | data formatting | bytes 131072
  40.9 0.3 copy-done.1
  41.1 12.0 %scatter_add.1 = f32[4,6912]{1,0:T(4,128)} custom-call(f32[1280,128]{1,0:T(8,128)S(1)} %bitcast.109, s32[1,128,256]{2,1,0:T(8,128)S(1)} %copy-done.1), custom_call_target="tpu_custom_call" | custom-call | tf_op jit(solution)/shard_map/scatter_add/pallas_call | solution.py:95
  (82 shorter events, 2.6 us)
Async XLA Ops:
  0.6 22.5 %copy-start = (f32[16,8,64]{2,1,0:T(8,128)S(1)}, f32[16,8,64]{2,1,0:T(8,128)}, u32[]{:S(2)}) copy-start(f32[16,8,64]{2,1,0:T(8,128)} %param.12) | copy-start | bytes 98308
  2.4 21.6 %collective-permute-start = (f32[65,3,64]{2,1,0:T(4,128)S(1)}, f32[65,3,64]{2,1,0:T(4,128)S(1)}, u32[]{:S(2)}, u32[]{:S(2)}) collective-permute-start(f32[65,3,64]{2,1,0:T(4,128)S(1)} %get-tuple-element.24), channel_id=1, source_target_pairs={{0,1},{1,2},{2,3},{4,5},{5,6},{6,7},{8,9},{9,10},{10,11},{12,13},{... | collective-permute-start | bytes 149768 | tf_op jit(solution)/shard_map/ppermute | solution.py:111
  6.5 17.6 %collective-permute-start.1 = (f32[65,3,64]{2,1,0:T(4,128)S(1)}, f32[65,3,64]{2,1,0:T(4,128)S(1)}, u32[]{:S(2)}, u32[]{:S(2)}) collective-permute-start(f32[65,3,64]{2,1,0:T(4,128)S(1)} %get-tuple-element.25), channel_id=1, source_target_pairs={{1,0},{2,1},{3,2},{5,4},{6,5},{7,6},{9,8},{10,9},{11,10},{13,12},{... | collective-permute-start | bytes 149768 | tf_op jit(solution)/shard_map/ppermute | solution.py:112
  11.1 29.7 %all-to-all-start = ((f32[128,1,1280]{2,1,0:T(1,128)}), f32[128,1,1280]{2,1,0:T(1,128)S(1)}, u32[]{:S(2)}, u32[]{:S(2)}) async-start(f32[128,1,1280]{2,1,0:T(1,128)} %bitcast.113), calls=%async_computation | async-start | bytes 1310720 | tf_op jit(solution)/shard_map/all_to_all | solution.py:185
  23.9 0.9 %copy-start.3 = (f32[2,16,8,64]{3,2,1,0:T(8,128)S(1)}, f32[2,16,8,64]{3,2,1,0:T(8,128)}, u32[]{:S(2)}) copy-start(f32[2,16,8,64]{3,2,1,0:T(8,128)} %tracers.1) | copy-start | bytes 196612
  23.9 0.9 %copy-start.4 = (f32[16,8,64]{2,1,0:T(8,128)S(1)}, f32[16,8,64]{2,1,0:T(8,128)}, u32[]{:S(2)}) copy-start(f32[16,8,64]{2,1,0:T(8,128)} %v_face.1) | copy-start | bytes 98308
  23.9 0.9 %copy-start.5 = (f32[16,8,64]{2,1,0:T(8,128)S(1)}, f32[16,8,64]{2,1,0:T(8,128)}, u32[]{:S(2)}) copy-start(f32[16,8,64]{2,1,0:T(8,128)} %u_face.1) | copy-start | bytes 98308
  25.4 6.3 %collective-permute-start.2 = (f32[65,14,3]{0,1,2:T(8,128)S(1)}, f32[65,14,3]{0,1,2:T(8,128)S(1)}, u32[]{:S(2)}, u32[]{:S(2)}) collective-permute-start(f32[65,14,3]{0,1,2:T(8,128)S(1)} %copy.67), channel_id=1, source_target_pairs={{0,4},{4,8},{8,12},{12,16},{16,20},{20,24},{24,28},{28,32},{32,36}... | collective-permute-start | bytes 32768 | tf_op jit(solution)/shard_map/ppermute | solution.py:111
  29.4 5.7 %collective-permute-start.3 = (f32[65,14,3]{0,1,2:T(8,128)S(1)}, f32[65,14,3]{0,1,2:T(8,128)S(1)}, u32[]{:S(2)}, u32[]{:S(2)}) collective-permute-start(f32[65,14,3]{0,1,2:T(8,128)S(1)} %copy.68), channel_id=1, source_target_pairs={{4,0},{8,4},{12,8},{16,12},{20,16},{24,20},{28,24},{32,28},{36,32}... | collective-permute-start | bytes 32768 | tf_op jit(solution)/shard_map/ppermute | solution.py:112
  35.9 0.8 %copy-start.2 = (f32[65,14,70]{2,1,0:T(8,128)}, f32[65,14,70]{2,1,0:T(8,128)S(1)}, u32[]{:S(2)}) copy-start(f32[65,14,70]{2,1,0:T(8,128)S(1)} %pad_maximum_fusion.1) | copy-start | bytes 764404
  37.1 1.0 %slice-start = ((f32[65,14,70]{2,1,0:T(8,128)}), f32[32,14,70]{2,1,0:T(8,128)S(1)}, s32[]{:S(2)}) async-start(f32[65,14,70]{2,1,0:T(8,128)} %copy-done.2), calls=%async_computation.1 | async-start | bytes 524288 | tf_op jit(solution)/shard_map/slice | solution.py:192
  40.2 1.0 %copy-start.1 = (s32[1,128,256]{2,1,0:T(8,128)S(1)}, s32[1,128,256]{2,1,0:T(8,128)}, u32[]{:S(2)}) copy-start(s32[1,128,256]{2,1,0:T(8,128)} %atm_cell.1) | copy-start | bytes 393220

commit v2 on v0

v2 whole, which is shorter than its diff:
```python
import functools

import jax
import jax.numpy as jnp
from jax import lax
from jax.experimental import pallas as pl
from jax.experimental.pallas import tpu as pltpu
from jax.sharding import PartitionSpec as P

A_DEV = 6912
HI = 27
PER = 4

def lanes_of(shape):
    return lax.broadcasted_iota(jnp.int32, shape, len(shape) - 1)

def wide(x, y=None):
    return jnp.concatenate([x, x if y is None else y], axis=1)

def strips_kernel(tracers, u_face, land_mask, to_east, to_west):
    lane = lanes_of((8, 128))
    spot = lane & 3
    east = jnp.zeros((8, 128), jnp.float32)
    west = jnp.zeros((8, 128), jnp.float32)
    wet = wide(land_mask[...].astype(jnp.float32))
    for p in range(32):
        here = lane >> 2 == p
        cells = wide(tracers[p // 16, p % 16])
        east = jnp.where(here, pltpu.roll(cells, (4 * p - 61) % 128, 1), east)
        west = jnp.where(here, pltpu.roll(cells, 4 * p, 1), west)
        last = 4 * p + 3
        if p < 16:
            east = jnp.where(lane == last, pltpu.roll(wide(u_face[p]), (last - 63) % 128, 1), east)
        elif p == 16:
            east = jnp.where(lane == last, pltpu.roll(wet, (last - 63) % 128, 1), east)
            west = jnp.where(lane == last, pltpu.roll(wet, last, 1), west)
    to_east[...] = east
    to_west[...] = west

def sweep(q, c, size, axis):
    def at(x, s):
        return pltpu.roll(x, (-s) % size, axis)
    nxt = at(q, 1)
    edge = (7.0 * (q + nxt) - (at(q, -1) + at(nxt, 1))) * (1.0 / 12.0)
    left = at(edge, -1)
    slope = edge - left
    curve = 6.0 * q - 3.0 * (left + edge)
    east = c >= 0.0
    size_c = jnp.abs(c)
    first = jnp.where(east, -slope, at(slope, 1))
    second = jnp.where(east, curve, at(curve, 1))
    flux = c * (edge + (0.5 * size_c) * (first + (1.0 - size_c * (2.0 / 3.0)) * second))
    return q - (flux - at(flux, -1))

def east_kernel(tracers, u_face, v_face, land_mask, from_west, from_east, swept, to_next, to_prev):
    lane = lanes_of((8, 128))
    own = lane < 64
    west_part = lane >= 96
    west = from_west[...]
    east = from_east[...]
    def put(cells, src, at_lane, lane_here, base):
        return jnp.where(lane == lane_here, pltpu.roll(src, (lane_here - at_lane) % 128, 1), base)
    wet = wide(land_mask[...].astype(jnp.float32))
    wet_x = put(None, west, 67, 127, put(None, east, 67, 64, wet))
    mm = wet_x * pltpu.roll(wet_x, 127, 1)
    for k in range(16):
        u = put(None, west, 4 * k + 3, 127, wide(u_face[k]))
        c = u * mm
        both = []
        for t in range(2):
            p = t * 16 + k
            halo = jnp.where(west_part, pltpu.roll(west, (125 - 4 * p) % 128, 1), pltpu.roll(east, (64 - 4 * p) % 128, 1))
            q = jnp.where(own, wide(tracers[t, k]), halo)
            both.append(sweep(q, c, 128, 1)[:, :64])
        z = wide(both[0], both[1])
        swept[k] = z
        to_next[k, 0:3, :] = z[5:8]
        to_prev[k, 0:3, :] = z[0:3]
        to_next[k, 3:4, :] = wide(v_face[k, 7:8, :], wet[7:8, :64])
        to_prev[k, 3:4, :] = wide(v_face[k, 0:1, :], wet[0:1, :64])

def north_kernel(swept, v_face, land_mask, thickness, from_prev, from_next, out):
    row = lax.broadcasted_iota(jnp.int32, (8, 128), 0)
    lane = lanes_of((8, 128))
    wet = wide(land_mask[...].astype(jnp.float32))
    def twin(x):
        return jnp.where(lane < 64, pltpu.roll(x, 64, 1), x)
    def eight(ref, k):
        x = ref[k]
        return jnp.concatenate([x, x], axis=0)
    prev0 = twin(eight(from_prev, 0)); next0 = twin(eight(from_next, 0))
    wet_y = jnp.concatenate([wet, jnp.where(row == 0, pltpu.roll(next0, (0 - 3) % 8, 0), prev0)], axis=0)
    mm = wet_y * pltpu.roll(wet_y, 15, 0)
    def flip(x):
        return jnp.where(lane < 64, x, pltpu.roll(x, 64, 1))
    z = []
    for k in range(16):
        prev = eight(from_prev, k)
        nxt = eight(from_next, k)
        v = jnp.concatenate([wide(v_face[k]), flip(prev)], axis=0)
        q = jnp.concatenate([swept[k], jnp.where(row < 4, nxt, pltpu.roll(prev, 1, 0))], axis=0)
        z.append(sweep(q, v * mm, 16, 0)[:8])
    tops = [jnp.zeros((8, 128), jnp.float32)]
    for j in range(16):
        tops.append(tops[-1] + wide(thickness[j]))
    thick = tops[16] * (1.0 / 16.0)
    inverse = 1.0 / thick
    for k in range(16):
        top = thick * float(k)
        base = thick * float(k + 1)
        total = jnp.zeros((8, 128), jnp.float32)
        for j in range(16):
            depth = jnp.maximum(jnp.minimum(tops[j + 1], base) - jnp.maximum(tops[j], top), 0.0)
            total = total + depth * z[j]
        total = total * inverse
        out[0, k] = total[:, :64]
        out[1, k] = total[:, 64:]

VM = pl.BlockSpec(memory_space=pltpu.VMEM)
def f32(*shape):
    return jax.ShapeDtypeStruct(shape, jnp.float32)
def call(kernel, name, outs, args):
    return pl.pallas_call(kernel, in_specs=[VM] * len(args), out_specs=[VM] * len(outs), out_shape=list(outs), compiler_params=pltpu.CompilerParams(vmem_limit_bytes=8 * 2**20), name=name)(*args)

def shift(x, axis, step):
    n = lax.axis_size(axis)
    pairs = [(i, i + 1) for i in range(n - 1)]
    if step < 0:
        pairs = [(j, i) for i, j in pairs]
    return lax.ppermute(x, axis, pairs)

def advect(tracers, u_face, v_face, thickness, land_mask):
    to_east, to_west = call(strips_kernel, "column_strips", [f32(8, 128)] * 2, (tracers, u_face, land_mask))
    from_west = shift(to_east, "gx", 1)
    from_east = shift(to_west, "gx", -1)
    swept, to_next, to_prev = call(east_kernel, "sweep_longitude", [f32(16, 8, 128), f32(16, 4, 128), f32(16, 4, 128)],
        (tracers, u_face, v_face, land_mask, from_west, from_east))
    from_prev = shift(to_next, "gy", 1)
    from_next = shift(to_prev, "gy", -1)
    return call(north_kernel, "sweep_latitude", [f32(2, 16, 8, 64)], (swept, v_face, land_mask, thickness, from_prev, from_next))[0]


def lane_take(table, lanes):
    return jnp.take_along_axis(table, lanes, axis=1, mode="promise_in_bounds")
def gather_kernel(tracers, u_face, v_face, land_mask, counts, ocean_cell, weight, payload):
    def packed(x):
        return jnp.concatenate([x[0:4, :], x[4:8, :]], axis=1)
    wet = packed(land_mask[...].astype(jnp.float32))
    east = packed(u_face[0]); north = packed(v_face[0])
    speed = jnp.sqrt(east * east + north * north + 0.01) * wet
    fields = [packed(tracers[0, 0]) * speed, packed(tracers[1, 0]) * speed, east * speed, north * speed, wet]
    tables = [[jnp.broadcast_to(f[q:q+1, :], (8, 128)) for q in range(4)] for f in fields]
    used = jnp.broadcast_to(counts[...], (8, 128))
    sub = lax.broadcasted_iota(jnp.int32, (8, 128), 0)
    lane_ids = lax.broadcasted_iota(jnp.int32, (8, 128), 1)
    def step(g, _):
        o = pl.multiple_of(g * 8, 8)
        count = lane_take(used, sub + o)
        for h in range(2):
            cell = ocean_cell[0, pl.ds(o, 8), h*128:(h+1)*128]
            share = jnp.where(lane_ids + h*128 < count, weight[0, pl.ds(o, 8), h*128:(h+1)*128], 0.0)
            lanes = (cell & 63) | ((cell >> 2) & 64)
            odd = (cell & 64) != 0
            upper = (cell & 128) != 0
            for f in range(5):
                a, b, c, d = [lane_take(t, lanes) for t in tables[f]]
                val = jnp.where(upper, jnp.where(odd, d, c), jnp.where(odd, b, a))
                payload[pl.ds(g * 80 + f*2+h, 8, stride=10), :] = val * share
        return 0
    lax.fori_loop(0, 16, step, 0, unroll=16)


def scatter_kernel(received, atm_cell, flux, fin):
    sub = lax.broadcasted_iota(jnp.int32, (16, 128), 0)
    def bf(x):
        return x.astype(jnp.float32).astype(jnp.bfloat16)
    low_ids = [bf(sub + 16 * k) for k in range(16)]
    high_ids = []
    for k in range(17):
        first = (16 * k) // HI
        row = sub + 16 * k - first * HI
        row = jnp.where(row >= HI, row - HI, row)
        if k == 16:
            row = jnp.where(sub < 14, row, -1)
        high_ids.append(bf(row))
    one, zero = jnp.bfloat16(1), jnp.bfloat16(0)
    def spread(row):
        return jnp.broadcast_to(row, (16, 128)).astype(jnp.bfloat16)
    def run(*accs):
        accs = [accs[:17], accs[17:]]
        for m in range(2):
            for a in accs[m]:
                pltpu.matmul_pop(a)
        def chunk(cells, pieces, s, mxu, stage):
            low = [spread((c[s:s+1] & 255).astype(jnp.float32)) for c in cells]
            rhs = jnp.concatenate([jnp.concatenate([jnp.where(lo == ids, one, zero) for lo in low], axis=1) for ids in low_ids], axis=0)
            pltpu.matmul_push_rhs(rhs, stage, mxu, transpose=True)
            high = [spread((c[s:s+1] >> 8).astype(jnp.float32)) for c in cells]
            tiles = {}
            for k in range(17):
                first = (16 * k) // HI
                edge = (first + 1) * HI - 16 * k
                for j in (first, first + 1):
                    if j < 10 and j not in tiles:
                        tiles[j] = [spread(p[s:s+1]) for p in pieces[j]]
                halves = []
                for h in range(2):
                    v = tiles[first][h]
                    if edge < 16 and first + 1 < 10:
                        v = jnp.where(sub < edge, v, tiles[first + 1][h])
                    halves.append(jnp.where(high[h] == high_ids[k], v, zero))
                pltpu.matmul_acc_lhs(accs[mxu][k], jnp.concatenate(halves, axis=1), load_staged_rhs=stage if k == 0 else None)
        def step(i, _):
            for k in range(PER):
                g = i * PER + k
                cells = [atm_cell[0, pl.ds(pl.multiple_of(g * 8, 8), 8), h*128:h*128+128] for h in range(2)]
                pieces = []
                for f in range(5):
                    val = [received[pl.ds(g * 80 + f*2+h, 8, stride=10), :] for h in range(2)]
                    top = [v.astype(jnp.bfloat16).astype(jnp.float32) for v in val]
                    pieces += [top, [v - t for v, t in zip(val, top)]]
                for s in range(8):
                    chunk(cells, pieces, s, s % 2, (s // 2) % 2)
            return 0
        lax.fori_loop(0, 16 // PER, step, 0)
        for k in range(17):
            total = pltpu.matmul_pop(accs[0][k]) + pltpu.matmul_pop(accs[1][k])
            for half in range(2):
                fin[half*272+k*16:half*272+k*16+16, :] = total[:, half*128:half*128+128]
    pl.run_scoped(run, *([pltpu.ACC(0)((16, 256), jnp.float32)] * 17 + [pltpu.ACC(1)((16, 256), jnp.float32)] * 17))
    for hi in range(27):
        for half in range(2):
            b = half * 272 + hi
            num = fin[pl.ds(b, 4, stride=54), :] + fin[pl.ds(b+27, 4, stride=54), :]
            den = fin[b+216:b+217, :] + fin[b+243:b+244, :]
            flux[:, hi*256+half*128:hi*256+half*128+128] = num / jnp.maximum(den, 0.2)


def gather(tracers, u_face, v_face, land_mask, counts, ocean_cell, weight):
    return pl.pallas_call(
        gather_kernel,
        grid=(1,),
        in_specs=[
            pl.BlockSpec((2, 1, 8, 64), lambda i: (0, 0, 0, 0)),
            pl.BlockSpec((1, 8, 64), lambda i: (0, 0, 0)),
            pl.BlockSpec((1, 8, 64), lambda i: (0, 0, 0)),
            pl.BlockSpec((8, 64), lambda i: (0, 0)),
            pl.BlockSpec((1, 128), lambda i: (0, 0)),
            pl.BlockSpec((1, 128, 256), lambda i: (0, 0, 0)),
            pl.BlockSpec((1, 128, 256), lambda i: (0, 0, 0)),
        ],
        out_specs=pl.BlockSpec((1280, 128), lambda i: (0, 0)),
        out_shape=f32(1280, 128),
        name="weighted_slots",
    )(tracers, u_face, v_face, land_mask, counts, ocean_cell, weight)


def scatter(received, atm_cell):
    return pl.pallas_call(
        scatter_kernel,
        in_specs=[VM] * 2,
        out_specs=VM,
        out_shape=f32(4, A_DEV),
        scratch_shapes=[pltpu.VMEM((544, 128), jnp.float32)],
        compiler_params=pltpu.CompilerParams(vmem_limit_bytes=16 * 2**20),
        name="owner_sums",
    )(received, atm_cell)


def on_device(tracers, u_face, v_face, thickness, land_mask, counts, ocean_cell, xgrid_weight, atm_cell):
    payload = gather(tracers, u_face, v_face, land_mask, counts, ocean_cell, xgrid_weight)
    received = lax.all_to_all(payload.reshape(128, 1, 1280), ("gx", "gy"), split_axis=0, concat_axis=0, tiled=True)
    tracers_new = advect(tracers, u_face, v_face, thickness, land_mask)
    atm_flux = scatter(received.reshape(1280, 128), atm_cell)
    return (tracers_new, atm_flux)


def solution(mesh):
    placed = (
        P(None, None, "gy", "gx"),
        P(None, "gy", "gx"),
        P(None, "gy", "gx"),
        P(None, "gy", "gx"),
        P("gy", "gx"),
        P(("gx", "gy"), None),
        P(("gx", "gy"), None, None),
        P(("gx", "gy"), None, None),
        P(("gx", "gy"), None, None),
    )
    return jax.shard_map(
        on_device,
        mesh=mesh,
        in_specs=placed,
        out_specs=(P(None, None, "gy", "gx"), P(None, ("gx", "gy"))),
        check_vma=False,
    )
```

time: 564 us -> 42.3 us (0.07)
  the two profiles are of different devices: /device:TPU:1 before, /device:TPU:6 now
where the time goes in v2:
time: 42.3 us; the launch traced here: 42 us
  starting transfers between devices  23.1 us (55%)
  Pallas kernels  11 us (26%)
  waiting for transfers between devices  7.14 us (17%)
  between operations  0.73 us (2%)
    ppermute x4, starting transfers between devices, shift(): return lax.ppermute(x, axis, pairs)  12.6 us
    all_to_all x1, starting transfers between devices, on_device(): lax.all_to_all(payload.reshape(128, 1, 1280), ('gx', 'gy'), split_axis=0,...  10.5 us
    ppermute x4, waiting for transfers between devices, shift(): return lax.ppermute(x, axis, pairs)  7.14 us
    pallas_call x1, Pallas kernels, scatter(): pl.pallas_call(scatter_kernel, in_specs=[VM] * 2, out_specs=VM, out_shape...  5.97 us
    pallas_call x1, Pallas kernels, gather(): pl.pallas_call(gather_kernel, grid=(1,), in_specs=[pl.BlockSpec((2, 1, 8,...  2.86 us
    pallas_call x3, Pallas kernels, call(): pl.pallas_call(kernel, in_specs=[VM] * len(args), out_specs=[VM] * len(ou...  2.17 us
  transfers between devices with their start and end apart: 5, of which 3 were waited for; matrix products, arithmetic and copies ran while one was open for 0% of the time, Pallas kernels for 5%

profile of v2, /device:TPU:6, one launch (start us, length us, event | category | flops | bytes accessed | tf_op | source)
XLA Modules:
  0.0 42.0 jit_solution(18100358451269507914)
XLA Ops:
  0.6 2.9 %weighted_slots.1 = f32[1280,128]{1,0:T(8,128)} custom-call(f32[2,16,8,64]{3,2,1,0:T(8,128)} %tracers.5, f32[16,8,64]{2,1,0:T(8,128)} %u_face.5, f32[16,8,64]{2,1,0:T(8,128)} %v_face.5, s32[8,64]{1,0:T(8,128)} %land_mask.7, s32[1,128]{1,0:T(1,128)} %counts.1, s32[1,128,256]{2,1,0:T(8,128)} %ocean_cell.1, f32[1,128,256]{2,1,0:T(8,128)} %weight.1), custom_call_target="tpu_custom_call" | custom-call | tf_op jit(solution)/shard_map/weighted_slots/pallas_call | solution.py:240
  3.5 0.0 copy-start
  3.5 10.5 %all-to-all-start = ((f32[128,1,1280]{2,1,0:T(1,128)}), f32[128,1,1280]{2,1,0:T(1,128)S(1)}, u32[]{:S(2)}, u32[]{:S(2)}) async-start(f32[128,1,1280]{2,1,0:T(1,128)} %bitcast.3), calls=%async_computation | async-start | bytes 1310720 | tf_op jit(solution)/shard_map/all_to_all | solution.py:272
  14.0 0.0 copy-done
  14.0 0.0 copy-done.1
  14.0 0.0 copy-done.4
  14.0 0.0 copy-start.2
  14.0 0.3 column_strips.1
  14.3 2.1 %collective-permute-start = (f32[8,128]{1,0:T(8,128)S(1)}, f32[8,128]{1,0:T(8,128)S(1)}, u32[]{:S(2)}, u32[]{:S(2)}) collective-permute-start(f32[8,128]{1,0:T(8,128)S(1)} %get-tuple-element.7), channel_id=1, source_target_pairs={{0,4},{4,8},{8,12},{12,16},{16,20},{20,24},{24,28},{28,32},{32,36}... | collective-permute-start | bytes 12296 | tf_op jit(solution)/shard_map/ppermute | solution.py:130
  16.3 0.0 copy-start.5
  16.4 5.7 %collective-permute-start.1 = (f32[8,128]{1,0:T(8,128)S(1)}, f32[8,128]{1,0:T(8,128)S(1)}, u32[]{:S(2)}, u32[]{:S(2)}) collective-permute-start(f32[8,128]{1,0:T(8,128)S(1)} %get-tuple-element.8), channel_id=1, source_target_pairs={{4,0},{8,4},{12,8},{16,12},{20,16},{24,20},{28,24},{32,28},{36,32}... | collective-permute-start | bytes 12296 | tf_op jit(solution)/shard_map/ppermute | solution.py:130
  22.1 2.6 %collective-permute-done.from_west = f32[8,128]{1,0:T(8,128)S(1)} collective-permute-done((f32[8,128]{1,0:T(8,128)S(1)}, f32[8,128]{1,0:T(8,128)S(1)}, u32[]{:S(2)}, u32[]{:S(2)}) %collective-permute-start) | collective-permute-done | bytes 4128 | tf_op jit(solution)/shard_map/ppermute | solution.py:130
  24.7 0.0 collective-permute-done.1.from_east
  24.7 0.0 copy-done.2
  24.7 0.8 %sweep_longitude.1 = (f32[16,8,128]{2,1,0:T(8,128)S(1)}, f32[16,4,128]{2,1,0:T(4,128)S(1)}, f32[16,4,128]{2,1,0:T(4,128)S(1)}) custom-call(f32[2,16,8,64]{3,2,1,0:T(8,128)S(1)} %copy-done, f32[16,8,64]{2,1,0:T(8,128)S(1)} %copy-done.1, f32[16,8,64]{2,1,0:T(8,128)S(1)} %copy-done.2, s32[8,64]{1,0:T(8,128)S(1)} %copy-done.4, ...), custom_call_target="tpu_custom_call" | custom-call | tf_op jit(solution)/shard_map/sweep_longitude/pallas_call | solution.py:123
  25.5 3.5 %collective-permute-start.2 = (f32[16,4,128]{2,1,0:T(4,128)S(1)}, f32[16,4,128]{2,1,0:T(4,128)S(1)}, u32[]{:S(2)}, u32[]{:S(2)}) collective-permute-start(f32[16,4,128]{2,1,0:T(4,128)S(1)} %get-tuple-element.10), channel_id=1, source_target_pairs={{0,1},{1,2},{2,3},{4,5},{5,6},{6,7},{8,9},{9,10},{10,11},{12,13},{... | collective-permute-start | bytes 98312 | tf_op jit(solution)/shard_map/ppermute | solution.py:130
  29.0 1.3 %collective-permute-start.3 = (f32[16,4,128]{2,1,0:T(4,128)S(1)}, f32[16,4,128]{2,1,0:T(4,128)S(1)}, u32[]{:S(2)}, u32[]{:S(2)}) collective-permute-start(f32[16,4,128]{2,1,0:T(4,128)S(1)} %get-tuple-element.11), channel_id=1, source_target_pairs={{1,0},{2,1},{3,2},{5,4},{6,5},{7,6},{9,8},{10,9},{11,10},{13,12},{... | collective-permute-start | bytes 98312 | tf_op jit(solution)/shard_map/ppermute | solution.py:130
  30.3 0.3 collective-permute-done.2.from_prev
  30.6 4.2 %collective-permute-done.3.from_next = f32[16,4,128]{2,1,0:T(4,128)S(1)} collective-permute-done((f32[16,4,128]{2,1,0:T(4,128)S(1)}, f32[16,4,128]{2,1,0:T(4,128)S(1)}, u32[]{:S(2)}, u32[]{:S(2)}) %collective-permute-start.3) | collective-permute-done | bytes 32800 | tf_op jit(solution)/shard_map/ppermute | solution.py:130
  34.8 0.0 copy-done.5
  34.8 1.1 %sweep_latitude.1 = f32[2,16,8,64]{3,2,1,0:T(8,128)} custom-call(f32[16,8,128]{2,1,0:T(8,128)S(1)} %get-tuple-element.9.swept, f32[16,8,64]{2,1,0:T(8,128)S(1)} %copy-done.2, s32[8,64]{1,0:T(8,128)S(1)} %copy-done.4, f32[16,8,64]{2,1,0:T(8,128)S(1)} %copy-done.5, f32[16,4,128]{2,1,0:T(4,128)S(1)} %collective-permute-done.2.from_prev, ...), custom_call_target="tpu_custom_call" | custom-call | tf_op jit(solution)/shard_map/sweep_latitude/pallas_call | solution.py:123
  36.0 0.0 all-to-all-done
  36.0 0.0 copy-done.3
  36.0 6.0 %owner_sums.1 = f32[4,6912]{1,0:T(4,128)} custom-call(f32[1280,128]{1,0:T(8,128)S(1)} %bitcast.2, s32[1,128,256]{2,1,0:T(8,128)S(1)} %copy-done.3), custom_call_target="tpu_custom_call" | custom-call | tf_op jit(solution)/shard_map/owner_sums/pallas_call | solution.py:259
  (3 shorter events, 0.0 us)
Async XLA Ops:
  3.5 10.5 %copy-start = (f32[2,16,8,64]{3,2,1,0:T(8,128)S(1)}, f32[2,16,8,64]{3,2,1,0:T(8,128)}, u32[]{:S(2)}) copy-start(f32[2,16,8,64]{3,2,1,0:T(8,128)} %tracers.5) | copy-start | bytes 196612
  3.5 10.5 %copy-start.1 = (f32[16,8,64]{2,1,0:T(8,128)S(1)}, f32[16,8,64]{2,1,0:T(8,128)}, u32[]{:S(2)}) copy-start(f32[16,8,64]{2,1,0:T(8,128)} %u_face.5) | copy-start | bytes 98308
  3.5 10.5 %copy-start.4 = (s32[8,64]{1,0:T(8,128)S(1)}, s32[8,64]{1,0:T(8,128)}, u32[]{:S(2)}) copy-start(s32[8,64]{1,0:T(8,128)} %land_mask.7) | copy-start | bytes 6148
  3.5 32.5 %all-to-all-start = ((f32[128,1,1280]{2,1,0:T(1,128)}), f32[128,1,1280]{2,1,0:T(1,128)S(1)}, u32[]{:S(2)}, u32[]{:S(2)}) async-start(f32[128,1,1280]{2,1,0:T(1,128)} %bitcast.3), calls=%async_computation | async-start | bytes 1310720 | tf_op jit(solution)/shard_map/all_to_all | solution.py:272
  14.0 10.7 %copy-start.2 = (f32[16,8,64]{2,1,0:T(8,128)S(1)}, f32[16,8,64]{2,1,0:T(8,128)}, u32[]{:S(2)}) copy-start(f32[16,8,64]{2,1,0:T(8,128)} %v_face.5) | copy-start | bytes 98308
  14.3 10.5 %collective-permute-start = (f32[8,128]{1,0:T(8,128)S(1)}, f32[8,128]{1,0:T(8,128)S(1)}, u32[]{:S(2)}, u32[]{:S(2)}) collective-permute-start(f32[8,128]{1,0:T(8,128)S(1)} %get-tuple-element.7), channel_id=1, source_target_pairs={{0,4},{4,8},{8,12},{12,16},{16,20},{20,24},{24,28},{28,32},{32,36}... | collective-permute-start | bytes 12296 | tf_op jit(solution)/shard_map/ppermute | solution.py:130
  16.3 18.5 %copy-start.5 = (f32[16,8,64]{2,1,0:T(8,128)S(1)}, f32[16,8,64]{2,1,0:T(8,128)}, u32[]{:S(2)}) copy-start(f32[16,8,64]{2,1,0:T(8,128)} %thickness.1) | copy-start | bytes 98308
  16.4 8.4 %collective-permute-start.1 = (f32[8,128]{1,0:T(8,128)S(1)}, f32[8,128]{1,0:T(8,128)S(1)}, u32[]{:S(2)}, u32[]{:S(2)}) collective-permute-start(f32[8,128]{1,0:T(8,128)S(1)} %get-tuple-element.8), channel_id=1, source_target_pairs={{4,0},{8,4},{12,8},{16,12},{20,16},{24,20},{28,24},{32,28},{36,32}... | collective-permute-start | bytes 12296 | tf_op jit(solution)/shard_map/ppermute | solution.py:130
  25.5 5.1 %collective-permute-start.2 = (f32[16,4,128]{2,1,0:T(4,128)S(1)}, f32[16,4,128]{2,1,0:T(4,128)S(1)}, u32[]{:S(2)}, u32[]{:S(2)}) collective-permute-start(f32[16,4,128]{2,1,0:T(4,128)S(1)} %get-tuple-element.10), channel_id=1, source_target_pairs={{0,1},{1,2},{2,3},{4,5},{5,6},{6,7},{8,9},{9,10},{10,11},{12,13},{... | collective-permute-start | bytes 98312 | tf_op jit(solution)/shard_map/ppermute | solution.py:130
  29.0 5.8 %collective-permute-start.3 = (f32[16,4,128]{2,1,0:T(4,128)S(1)}, f32[16,4,128]{2,1,0:T(4,128)S(1)}, u32[]{:S(2)}, u32[]{:S(2)}) collective-permute-start(f32[16,4,128]{2,1,0:T(4,128)S(1)} %get-tuple-element.11), channel_id=1, source_target_pairs={{1,0},{2,1},{3,2},{5,4},{6,5},{7,6},{9,8},{10,9},{11,10},{13,12},{... | collective-permute-start | bytes 98312 | tf_op jit(solution)/shard_map/ppermute | solution.py:130
  34.8 1.2 %copy-start.3 = (s32[1,128,256]{2,1,0:T(8,128)S(1)}, s32[1,128,256]{2,1,0:T(8,128)}, u32[]{:S(2)}) copy-start(s32[1,128,256]{2,1,0:T(8,128)} %atm_cell.1) | copy-start | bytes 393220

commit v3 on v2

--- a/solution.py
+++ b/solution.py
@@ -129,15 +129,22 @@
         pairs = [(j, i) for i, j in pairs]
     return lax.ppermute(x, axis, pairs)
 
-def advect(tracers, u_face, v_face, thickness, land_mask):
-    to_east, to_west = call(strips_kernel, "column_strips", [f32(8, 128)] * 2, (tracers, u_face, land_mask))
-    from_west = shift(to_east, "gx", 1)
-    from_east = shift(to_west, "gx", -1)
-    swept, to_next, to_prev = call(east_kernel, "sweep_longitude", [f32(16, 8, 128), f32(16, 4, 128), f32(16, 4, 128)],
-        (tracers, u_face, v_face, land_mask, from_west, from_east))
-    from_prev = shift(to_next, "gy", 1)
-    from_next = shift(to_prev, "gy", -1)
-    return call(north_kernel, "sweep_latitude", [f32(2, 16, 8, 64)], (swept, v_face, land_mask, thickness, from_prev, from_next))[0]
+def strips(tracers, u_face, land_mask):
+    return call(strips_kernel, "column_strips", [f32(8, 128)] * 2, (tracers, u_face, land_mask))
+
+
+def longitude(tracers, u_face, v_face, land_mask, from_west, from_east):
+    return call(
+        east_kernel,
+        "sweep_longitude",
+        [f32(16, 8, 128), f32(16, 4, 128), f32(16, 4, 128)],
+        (tracers, u_face, v_face, land_mask, from_west, from_east),
+    )
+
+
+def latitude(swept, v_face, land_mask, thickness, from_prev, from_next):
+    args = (swept, v_face, land_mask, thickness, from_prev, from_next)
+    return call(north_kernel, "sweep_latitude", [f32(2, 16, 8, 64)], args)[0]
 
 
 def lane_take(table, lanes):
@@ -270,8 +277,16 @@
 def on_device(tracers, u_face, v_face, thickness, land_mask, counts, ocean_cell, xgrid_weight, atm_cell):
     payload = gather(tracers, u_face, v_face, land_mask, counts, ocean_cell, xgrid_weight)
     received = lax.all_to_all(payload.reshape(128, 1, 1280), ("gx", "gy"), split_axis=0, concat_axis=0, tiled=True)
-    tracers_new = advect(tracers, u_face, v_face, thickness, land_mask)
+    to_east, to_west = strips(tracers, u_face, land_mask)
+    from_west = shift(to_east, "gx", 1)
+    from_east = shift(to_west, "gx", -1)
+    swept, to_next, to_prev = longitude(tracers, u_face, v_face, land_mask, from_west, from_east)
+    received, _ = lax.optimization_barrier((received, to_next))
+    from_prev = shift(to_next, "gy", 1)
+    from_next = shift(to_prev, "gy", -1)
     atm_flux = scatter(received.reshape(1280, 128), atm_cell)
+    atm_flux, from_prev, from_next = lax.optimization_barrier((atm_flux, from_prev, from_next))
+    tracers_new = latitude(swept, v_face, land_mask, thickness, from_prev, from_next)
     return (tracers_new, atm_flux)
 
 

time: 42.3 us -> 38.8 us (0.917)
  the two profiles are of different devices: /device:TPU:6 before, /device:TPU:14 now
where the time goes in v3:
time: 38.8 us; the launch traced here: 38.5 us
  starting transfers between devices  24 us (62%)
  Pallas kernels  11 us (28%)
  waiting for transfers between devices  2.75 us (7%)
  between operations  0.75 us (2%)
    ppermute x4, starting transfers between devices, shift(): return lax.ppermute(x, axis, pairs)  13.6 us
    all_to_all x1, starting transfers between devices, on_device(): lax.all_to_all(payload.reshape(128, 1, 1280), ('gx', 'gy'), split_axis=0,...  10.4 us
    pallas_call x1, Pallas kernels, scatter(): pl.pallas_call(scatter_kernel, in_specs=[VM] * 2, out_specs=VM, out_shape...  5.97 us
    pallas_call x1, Pallas kernels, gather(): pl.pallas_call(gather_kernel, grid=(1,), in_specs=[pl.BlockSpec((2, 1, 8,...  2.86 us
    ppermute x4, waiting for transfers between devices, shift(): return lax.ppermute(x, axis, pairs)  2.75 us
    pallas_call x3, Pallas kernels, call(): pl.pallas_call(kernel, in_specs=[VM] * len(args), out_specs=[VM] * len(ou...  2.17 us
  transfers between devices with their start and end apart: 5, of which 1 were waited for; matrix products, arithmetic and copies ran while one was open for 0% of the time, Pallas kernels for 18%

profile of v3, /device:TPU:14, one launch (start us, length us, event | category | flops | bytes accessed | tf_op | source)
XLA Modules:
  0.0 38.5 jit_solution(7772833192485878978)
XLA Ops:
  0.6 2.9 %weighted_slots.1 = f32[1280,128]{1,0:T(8,128)} custom-call(f32[2,16,8,64]{3,2,1,0:T(8,128)} %tracers.5, f32[16,8,64]{2,1,0:T(8,128)} %u_face.5, f32[16,8,64]{2,1,0:T(8,128)} %v_face.5, s32[8,64]{1,0:T(8,128)} %land_mask.7, s32[1,128]{1,0:T(1,128)} %counts.1, s32[1,128,256]{2,1,0:T(8,128)} %ocean_cell.1, f32[1,128,256]{2,1,0:T(8,128)} %weight.1), custom_call_target="tpu_custom_call" | custom-call | tf_op jit(solution)/shard_map/weighted_slots/pallas_call | solution.py:247
  3.5 10.4 %all-to-all-start = ((f32[128,1,1280]{2,1,0:T(1,128)}), f32[128,1,1280]{2,1,0:T(1,128)S(1)}, u32[]{:S(2)}, u32[]{:S(2)}) async-start(f32[128,1,1280]{2,1,0:T(1,128)} %bitcast.3), calls=%async_computation | async-start | bytes 1310720 | tf_op jit(solution)/shard_map/all_to_all | solution.py:279
  13.9 0.0 copy-done
  13.9 0.0 copy-done.1
  13.9 0.0 copy-done.4
  13.9 0.0 copy-start.2
  13.9 0.3 column_strips.1
  14.2 2.1 %collective-permute-start = (f32[8,128]{1,0:T(8,128)S(1)}, f32[8,128]{1,0:T(8,128)S(1)}, u32[]{:S(2)}, u32[]{:S(2)}) collective-permute-start(f32[8,128]{1,0:T(8,128)S(1)} %get-tuple-element.11), channel_id=1, source_target_pairs={{0,4},{4,8},{8,12},{12,16},{16,20},{20,24},{24,28},{28,32},{32,36}... | collective-permute-start | bytes 12296 | tf_op jit(solution)/shard_map/ppermute | solution.py:130
  16.2 0.0 copy-start.3
  16.2 5.7 %collective-permute-start.1 = (f32[8,128]{1,0:T(8,128)S(1)}, f32[8,128]{1,0:T(8,128)S(1)}, u32[]{:S(2)}, u32[]{:S(2)}) collective-permute-start(f32[8,128]{1,0:T(8,128)S(1)} %get-tuple-element.12), channel_id=1, source_target_pairs={{4,0},{8,4},{12,8},{16,12},{20,16},{24,20},{28,24},{32,28},{36,32}... | collective-permute-start | bytes 12296 | tf_op jit(solution)/shard_map/ppermute | solution.py:130
  22.0 2.7 %collective-permute-done.from_west = f32[8,128]{1,0:T(8,128)S(1)} collective-permute-done((f32[8,128]{1,0:T(8,128)S(1)}, f32[8,128]{1,0:T(8,128)S(1)}, u32[]{:S(2)}, u32[]{:S(2)}) %collective-permute-start) | collective-permute-done | bytes 4128 | tf_op jit(solution)/shard_map/ppermute | solution.py:130
  24.7 0.0 collective-permute-done.1.from_east
  24.7 0.0 copy-done.2
  24.8 0.8 %sweep_longitude.1 = (f32[16,8,128]{2,1,0:T(8,128)S(1)}, f32[16,4,128]{2,1,0:T(4,128)S(1)}, f32[16,4,128]{2,1,0:T(4,128)S(1)}) custom-call(f32[2,16,8,64]{3,2,1,0:T(8,128)S(1)} %copy-done, f32[16,8,64]{2,1,0:T(8,128)S(1)} %copy-done.1, f32[16,8,64]{2,1,0:T(8,128)S(1)} %copy-done.2, s32[8,64]{1,0:T(8,128)S(1)} %copy-done.4, ...), custom_call_target="tpu_custom_call" | custom-call | tf_op jit(solution)/shard_map/sweep_longitude/pallas_call | solution.py:123
  25.5 3.4 %collective-permute-start.2 = (f32[16,4,128]{2,1,0:T(4,128)S(1)}, f32[16,4,128]{2,1,0:T(4,128)S(1)}, u32[]{:S(2)}, u32[]{:S(2)}) collective-permute-start(f32[16,4,128]{2,1,0:T(4,128)S(1)} %get-tuple-element.14), channel_id=1, source_target_pairs={{0,1},{1,2},{2,3},{4,5},{5,6},{6,7},{8,9},{9,10},{10,11},{12,13},{... | collective-permute-start | bytes 98312 | tf_op jit(solution)/shard_map/ppermute | solution.py:130
  28.9 2.5 %collective-permute-start.3 = (f32[16,4,128]{2,1,0:T(4,128)S(1)}, f32[16,4,128]{2,1,0:T(4,128)S(1)}, u32[]{:S(2)}, u32[]{:S(2)}) collective-permute-start(f32[16,4,128]{2,1,0:T(4,128)S(1)} %get-tuple-element.16), channel_id=1, source_target_pairs={{1,0},{2,1},{3,2},{5,4},{6,5},{7,6},{9,8},{10,9},{11,10},{13,12},{... | collective-permute-start | bytes 98312 | tf_op jit(solution)/shard_map/ppermute | solution.py:130
  31.4 0.0 all-to-all-done
  31.4 0.0 copy-done.3
  31.4 0.0 copy-start.5
  31.4 6.0 %owner_sums.1 = f32[4,6912]{1,0:T(4,128)} custom-call(f32[1280,128]{1,0:T(8,128)S(1)} %bitcast.2, s32[1,128,256]{2,1,0:T(8,128)S(1)} %copy-done.3), custom_call_target="tpu_custom_call" | custom-call | tf_op jit(solution)/shard_map/owner_sums/pallas_call | solution.py:266
  37.4 0.0 collective-permute-done.2.from_prev
  37.4 0.0 collective-permute-done.3.from_next
  37.4 0.0 copy-done.5
  37.4 1.1 %sweep_latitude.1 = f32[2,16,8,64]{3,2,1,0:T(8,128)} custom-call(f32[16,8,128]{2,1,0:T(8,128)S(1)} %get-tuple-element.13.swept, f32[16,8,64]{2,1,0:T(8,128)S(1)} %copy-done.2, s32[8,64]{1,0:T(8,128)S(1)} %copy-done.4, f32[16,8,64]{2,1,0:T(8,128)S(1)} %copy-done.5, f32[16,4,128]{2,1,0:T(4,128)S(1)} %collective-permute-done.2.from_prev, ...), custom_call_target="tpu_custom_call" | custom-call | tf_op jit(solution)/shard_map/sweep_latitude/pallas_call | solution.py:123
  (3 shorter events, 0.0 us)
Async XLA Ops:
  3.5 10.4 %copy-start = (f32[2,16,8,64]{3,2,1,0:T(8,128)S(1)}, f32[2,16,8,64]{3,2,1,0:T(8,128)}, u32[]{:S(2)}) copy-start(f32[2,16,8,64]{3,2,1,0:T(8,128)} %tracers.5) | copy-start | bytes 196612
  3.5 10.4 %copy-start.1 = (f32[16,8,64]{2,1,0:T(8,128)S(1)}, f32[16,8,64]{2,1,0:T(8,128)}, u32[]{:S(2)}) copy-start(f32[16,8,64]{2,1,0:T(8,128)} %u_face.5) | copy-start | bytes 98308
  3.5 10.4 %copy-start.4 = (s32[8,64]{1,0:T(8,128)S(1)}, s32[8,64]{1,0:T(8,128)}, u32[]{:S(2)}) copy-start(s32[8,64]{1,0:T(8,128)} %land_mask.7) | copy-start | bytes 6148
  3.5 27.9 %all-to-all-start = ((f32[128,1,1280]{2,1,0:T(1,128)}), f32[128,1,1280]{2,1,0:T(1,128)S(1)}, u32[]{:S(2)}, u32[]{:S(2)}) async-start(f32[128,1,1280]{2,1,0:T(1,128)} %bitcast.3), calls=%async_computation | async-start | bytes 1310720 | tf_op jit(solution)/shard_map/all_to_all | solution.py:279
  13.9 10.8 %copy-start.2 = (f32[16,8,64]{2,1,0:T(8,128)S(1)}, f32[16,8,64]{2,1,0:T(8,128)}, u32[]{:S(2)}) copy-start(f32[16,8,64]{2,1,0:T(8,128)} %v_face.5) | copy-start | bytes 98308
  14.2 10.6 %collective-permute-start = (f32[8,128]{1,0:T(8,128)S(1)}, f32[8,128]{1,0:T(8,128)S(1)}, u32[]{:S(2)}, u32[]{:S(2)}) collective-permute-start(f32[8,128]{1,0:T(8,128)S(1)} %get-tuple-element.11), channel_id=1, source_target_pairs={{0,4},{4,8},{8,12},{12,16},{16,20},{20,24},{24,28},{28,32},{32,36}... | collective-permute-start | bytes 12296 | tf_op jit(solution)/shard_map/ppermute | solution.py:130
  16.2 15.2 %copy-start.3 = (s32[1,128,256]{2,1,0:T(8,128)S(1)}, s32[1,128,256]{2,1,0:T(8,128)}, u32[]{:S(2)}) copy-start(s32[1,128,256]{2,1,0:T(8,128)} %atm_cell.1) | copy-start | bytes 393220
  16.2 8.5 %collective-permute-start.1 = (f32[8,128]{1,0:T(8,128)S(1)}, f32[8,128]{1,0:T(8,128)S(1)}, u32[]{:S(2)}, u32[]{:S(2)}) collective-permute-start(f32[8,128]{1,0:T(8,128)S(1)} %get-tuple-element.12), channel_id=1, source_target_pairs={{4,0},{8,4},{12,8},{16,12},{20,16},{24,20},{28,24},{32,28},{36,32}... | collective-permute-start | bytes 12296 | tf_op jit(solution)/shard_map/ppermute | solution.py:130
  25.5 11.9 %collective-permute-start.2 = (f32[16,4,128]{2,1,0:T(4,128)S(1)}, f32[16,4,128]{2,1,0:T(4,128)S(1)}, u32[]{:S(2)}, u32[]{:S(2)}) collective-permute-start(f32[16,4,128]{2,1,0:T(4,128)S(1)} %get-tuple-element.14), channel_id=1, source_target_pairs={{0,1},{1,2},{2,3},{4,5},{5,6},{6,7},{8,9},{9,10},{10,11},{12,13},{... | collective-permute-start | bytes 98312 | tf_op jit(solution)/shard_map/ppermute | solution.py:130
  28.9 8.5 %collective-permute-start.3 = (f32[16,4,128]{2,1,0:T(4,128)S(1)}, f32[16,4,128]{2,1,0:T(4,128)S(1)}, u32[]{:S(2)}, u32[]{:S(2)}) collective-permute-start(f32[16,4,128]{2,1,0:T(4,128)S(1)} %get-tuple-element.16), channel_id=1, source_target_pairs={{1,0},{2,1},{3,2},{5,4},{6,5},{7,6},{9,8},{10,9},{11,10},{13,12},{... | collective-permute-start | bytes 98312 | tf_op jit(solution)/shard_map/ppermute | solution.py:130
  31.4 6.0 %copy-start.5 = (f32[16,8,64]{2,1,0:T(8,128)S(1)}, f32[16,8,64]{2,1,0:T(8,128)}, u32[]{:S(2)}) copy-start(f32[16,8,64]{2,1,0:T(8,128)} %thickness.1) | copy-start | bytes 98308

commit v4 on v3

--- a/solution.py
+++ b/solution.py
@@ -9,7 +9,7 @@
 
 A_DEV = 6912
 HI = 27
-PER = 4
+PER = 8
 
 def lanes_of(shape):
     return lax.broadcasted_iota(jnp.int32, shape, len(shape) - 1)
@@ -17,7 +17,11 @@
 def wide(x, y=None):
     return jnp.concatenate([x, x if y is None else y], axis=1)
 
-def strips_kernel(tracers, u_face, land_mask, to_east, to_west):
+def even_index(axis):
+    return lax.rem(lax.axis_index(axis), 2) == 0
+
+
+def strips_kernel(tracers, u_face, land_mask, to_near, to_far):
     lane = lanes_of((8, 128))
     spot = lane & 3
     east = jnp.zeros((8, 128), jnp.float32)
@@ -34,8 +38,9 @@
         elif p == 16:
             east = jnp.where(lane == last, pltpu.roll(wet, (last - 63) % 128, 1), east)
             west = jnp.where(lane == last, pltpu.roll(wet, last, 1), west)
-    to_east[...] = east
-    to_west[...] = west
+    even = even_index("gx")
+    to_near[...] = jnp.where(even, east, west)
+    to_far[...] = jnp.where(even, west, east)
 
 def sweep(q, c, size, axis):
     def at(x, s):
@@ -52,12 +57,14 @@
     flux = c * (edge + (0.5 * size_c) * (first + (1.0 - size_c * (2.0 / 3.0)) * second))
     return q - (flux - at(flux, -1))
 
-def east_kernel(tracers, u_face, v_face, land_mask, from_west, from_east, swept, to_next, to_prev):
+def east_kernel(tracers, u_face, v_face, land_mask, from_near, from_far, swept, to_pair, to_other):
+    even_row = even_index("gy")
     lane = lanes_of((8, 128))
     own = lane < 64
     west_part = lane >= 96
-    west = from_west[...]
-    east = from_east[...]
+    even = even_index("gx")
+    west = jnp.where(even, from_far[...], from_near[...])
+    east = jnp.where(even, from_near[...], from_far[...])
     def put(cells, src, at_lane, lane_here, base):
         return jnp.where(lane == lane_here, pltpu.roll(src, (lane_here - at_lane) % 128, 1), base)
     wet = wide(land_mask[...].astype(jnp.float32))
@@ -74,29 +81,33 @@
             both.append(sweep(q, c, 128, 1)[:, :64])
         z = wide(both[0], both[1])
         swept[k] = z
-        to_next[k, 0:3, :] = z[5:8]
-        to_prev[k, 0:3, :] = z[0:3]
-        to_next[k, 3:4, :] = wide(v_face[k, 7:8, :], wet[7:8, :64])
-        to_prev[k, 3:4, :] = wide(v_face[k, 0:1, :], wet[0:1, :64])
-
-def north_kernel(swept, v_face, land_mask, thickness, from_prev, from_next, out):
+        last = (z[5:8], wide(v_face[k, 7:8, :], wet[7:8, :64]))
+        first = (z[0:3], wide(v_face[k, 0:1, :], wet[0:1, :64]))
+        for rows, a, b in ((slice(0, 3), last[0], first[0]), (slice(3, 4), last[1], first[1])):
+            to_pair[k, rows, :] = jnp.where(even_row, a, b)
+            to_other[k, rows, :] = jnp.where(even_row, b, a)
+
+
+def north_kernel(swept, v_face, land_mask, thickness, from_pair, from_other, out):
+    even_row = even_index("gy")
     row = lax.broadcasted_iota(jnp.int32, (8, 128), 0)
     lane = lanes_of((8, 128))
     wet = wide(land_mask[...].astype(jnp.float32))
     def twin(x):
         return jnp.where(lane < 64, pltpu.roll(x, 64, 1), x)
-    def eight(ref, k):
-        x = ref[k]
-        return jnp.concatenate([x, x], axis=0)
-    prev0 = twin(eight(from_prev, 0)); next0 = twin(eight(from_next, 0))
+    def halos(k):
+        pair, other = from_pair[k], from_other[k]
+        prev, nxt = jnp.where(even_row, other, pair), jnp.where(even_row, pair, other)
+        return jnp.concatenate([prev, prev], axis=0), jnp.concatenate([nxt, nxt], axis=0)
+
+    prev0, next0 = [twin(x) for x in halos(0)]
     wet_y = jnp.concatenate([wet, jnp.where(row == 0, pltpu.roll(next0, (0 - 3) % 8, 0), prev0)], axis=0)
     mm = wet_y * pltpu.roll(wet_y, 15, 0)
     def flip(x):
         return jnp.where(lane < 64, x, pltpu.roll(x, 64, 1))
     z = []
     for k in range(16):
-        prev = eight(from_prev, k)
-        nxt = eight(from_next, k)
+        prev, nxt = halos(k)
         v = jnp.concatenate([wide(v_face[k]), flip(prev)], axis=0)
         q = jnp.concatenate([swept[k], jnp.where(row < 4, nxt, pltpu.roll(prev, 1, 0))], axis=0)
         z.append(sweep(q, v * mm, 16, 0)[:8])
@@ -122,28 +133,27 @@
 def call(kernel, name, outs, args):
     return pl.pallas_call(kernel, in_specs=[VM] * len(args), out_specs=[VM] * len(outs), out_shape=list(outs), compiler_params=pltpu.CompilerParams(vmem_limit_bytes=8 * 2**20), name=name)(*args)
 
-def shift(x, axis, step):
+def swap(x, axis, first):
     n = lax.axis_size(axis)
-    pairs = [(i, i + 1) for i in range(n - 1)]
-    if step < 0:
-        pairs = [(j, i) for i, j in pairs]
-    return lax.ppermute(x, axis, pairs)
+    pairs = [(i, i + 1) for i in range(first, n - 1, 2)]
+    return lax.ppermute(x, axis, pairs + [(j, i) for i, j in pairs])
+
 
 def strips(tracers, u_face, land_mask):
     return call(strips_kernel, "column_strips", [f32(8, 128)] * 2, (tracers, u_face, land_mask))
 
 
-def longitude(tracers, u_face, v_face, land_mask, from_west, from_east):
+def longitude(tracers, u_face, v_face, land_mask, from_near, from_far):
     return call(
         east_kernel,
         "sweep_longitude",
         [f32(16, 8, 128), f32(16, 4, 128), f32(16, 4, 128)],
-        (tracers, u_face, v_face, land_mask, from_west, from_east),
+        (tracers, u_face, v_face, land_mask, from_near, from_far),
     )
 
 
-def latitude(swept, v_face, land_mask, thickness, from_prev, from_next):
-    args = (swept, v_face, land_mask, thickness, from_prev, from_next)
+def latitude(swept, v_face, land_mask, thickness, from_pair, from_other):
+    args = (swept, v_face, land_mask, thickness, from_pair, from_other)
     return call(north_kernel, "sweep_latitude", [f32(2, 16, 8, 64)], args)[0]
 
 
@@ -277,16 +287,16 @@
 def on_device(tracers, u_face, v_face, thickness, land_mask, counts, ocean_cell, xgrid_weight, atm_cell):
     payload = gather(tracers, u_face, v_face, land_mask, counts, ocean_cell, xgrid_weight)
     received = lax.all_to_all(payload.reshape(128, 1, 1280), ("gx", "gy"), split_axis=0, concat_axis=0, tiled=True)
-    to_east, to_west = strips(tracers, u_face, land_mask)
-    from_west = shift(to_east, "gx", 1)
-    from_east = shift(to_west, "gx", -1)
-    swept, to_next, to_prev = longitude(tracers, u_face, v_face, land_mask, from_west, from_east)
-    received, _ = lax.optimization_barrier((received, to_next))
-    from_prev = shift(to_next, "gy", 1)
-    from_next = shift(to_prev, "gy", -1)
+    to_near, to_far = strips(tracers, u_face, land_mask)
+    from_far = swap(to_far, "gx", 1)
+    from_near = swap(to_near, "gx", 0)
+    swept, to_pair, to_other = longitude(tracers, u_face, v_face, land_mask, from_near, from_far)
+    received, _ = lax.optimization_barrier((received, to_pair))
+    from_other = swap(to_other, "gy", 1)
+    from_pair = swap(to_pair, "gy", 0)
     atm_flux = scatter(received.reshape(1280, 128), atm_cell)
-    atm_flux, from_prev, from_next = lax.optimization_barrier((atm_flux, from_prev, from_next))
-    tracers_new = latitude(swept, v_face, land_mask, thickness, from_prev, from_next)
+    atm_flux, from_pair, from_other = lax.optimization_barrier((atm_flux, from_pair, from_other))
+    tracers_new = latitude(swept, v_face, land_mask, thickness, from_pair, from_other)
     return (tracers_new, atm_flux)
 
 

time: 38.8 us -> 37.7 us (0.972)
  the two profiles are of different devices: /device:TPU:14 before, /device:TPU:1 now
where the time goes in v4:
time: 37.7 us; the launch traced here: 37.5 us
  starting transfers between devices  16.8 us (45%)
  Pallas kernels  10.7 us (28%)
  waiting for transfers between devices  9.27 us (25%)
  between operations  0.72 us (2%)
    all_to_all x1, starting transfers between devices, on_device(): lax.all_to_all(payload.reshape(128, 1, 1280), ('gx', 'gy'), split_axis=0,...  11.5 us
    all_to_all x1, waiting for transfers between devices, on_device(): lax.all_to_all(payload.reshape(128, 1, 1280), ('gx', 'gy'), split_axis=0,...  6.58 us
    pallas_call x1, Pallas kernels, scatter(): pl.pallas_call(scatter_kernel, in_specs=[VM] * 2, out_specs=VM, out_shape...  5.71 us
    ppermute x4, starting transfers between devices, swap(): return lax.ppermute(x, axis, pairs + [(j, i) for i, j in pairs])  5.28 us
    pallas_call x1, Pallas kernels, gather(): pl.pallas_call(gather_kernel, grid=(1,), in_specs=[pl.BlockSpec((2, 1, 8,...  2.86 us
    ppermute x4, waiting for transfers between devices, swap(): return lax.ppermute(x, axis, pairs + [(j, i) for i, j in pairs])  2.69 us
    pallas_call x3, Pallas kernels, call(): pl.pallas_call(kernel, in_specs=[VM] * len(args), out_specs=[VM] * len(ou...  2.13 us
  transfers between devices with their start and end apart: 5, of which 2 were waited for; matrix products, arithmetic and copies ran while one was open for 0% of the time, Pallas kernels for 18%

profile of v4, /device:TPU:1, one launch (start us, length us, event | category | flops | bytes accessed | tf_op | source)
XLA Modules:
  0.0 37.5 jit_solution(609337443818548489)
XLA Ops:
  0.6 2.9 %weighted_slots.1 = f32[1280,128]{1,0:T(8,128)} custom-call(f32[2,16,8,64]{3,2,1,0:T(8,128)} %tracers.5, f32[16,8,64]{2,1,0:T(8,128)} %u_face.5, f32[16,8,64]{2,1,0:T(8,128)} %v_face.5, s32[8,64]{1,0:T(8,128)} %land_mask.7, s32[1,128]{1,0:T(1,128)} %counts.1, s32[1,128,256]{2,1,0:T(8,128)} %ocean_cell.1, f32[1,128,256]{2,1,0:T(8,128)} %weight.1), custom_call_target="tpu_custom_call" | custom-call | tf_op jit(solution)/shard_map/weighted_slots/pallas_call | solution.py:257
  3.5 0.0 copy-start
  3.5 0.0 copy-start.1
  3.5 11.5 %all-to-all-start = ((f32[128,1,1280]{2,1,0:T(1,128)}), f32[128,1,1280]{2,1,0:T(1,128)S(1)}, u32[]{:S(2)}, u32[]{:S(2)}) async-start(f32[128,1,1280]{2,1,0:T(1,128)} %bitcast.3), calls=%async_computation | async-start | bytes 1310720 | tf_op jit(solution)/shard_map/all_to_all | solution.py:289
  15.0 0.0 copy-done
  15.0 0.0 copy-done.1
  15.0 0.0 copy-done.4
  15.0 0.0 copy-start.2
  15.1 0.3 column_strips.1
  15.3 1.1 %collective-permute-start = (f32[8,128]{1,0:T(8,128)S(1)}, f32[8,128]{1,0:T(8,128)S(1)}, u32[]{:S(2)}, u32[]{:S(2)}) collective-permute-start(f32[8,128]{1,0:T(8,128)S(1)} %get-tuple-element.11), channel_id=1, source_target_pairs={{0,4},{8,12},{16,20},{24,28},{32,36},{40,44},{48,52},{56,60},{64,6... | collective-permute-start | bytes 12296 | tf_op jit(solution)/shard_map/ppermute | solution.py:139
  16.5 2.9 %collective-permute-start.1 = (f32[8,128]{1,0:T(8,128)S(1)}, f32[8,128]{1,0:T(8,128)S(1)}, u32[]{:S(2)}, u32[]{:S(2)}) collective-permute-start(f32[8,128]{1,0:T(8,128)S(1)} %get-tuple-element.12), channel_id=1, source_target_pairs={{4,8},{12,16},{20,24},{28,32},{36,40},{44,48},{52,56},{60,64},{68,... | collective-permute-start | bytes 12296 | tf_op jit(solution)/shard_map/ppermute | solution.py:139
  19.3 0.0 collective-permute-done.from_near
  19.3 2.7 %collective-permute-done.1.from_far = f32[8,128]{1,0:T(8,128)S(1)} collective-permute-done((f32[8,128]{1,0:T(8,128)S(1)}, f32[8,128]{1,0:T(8,128)S(1)}, u32[]{:S(2)}, u32[]{:S(2)}) %collective-permute-start.1) | collective-permute-done | bytes 4128 | tf_op jit(solution)/shard_map/ppermute | solution.py:139
  22.0 0.0 copy-done.2
  22.0 0.7 %sweep_longitude.1 = (f32[16,8,128]{2,1,0:T(8,128)S(1)}, f32[16,4,128]{2,1,0:T(4,128)S(1)}, f32[16,4,128]{2,1,0:T(4,128)S(1)}) custom-call(f32[2,16,8,64]{3,2,1,0:T(8,128)S(1)} %copy-done, f32[16,8,64]{2,1,0:T(8,128)S(1)} %copy-done.1, f32[16,8,64]{2,1,0:T(8,128)S(1)} %copy-done.2, s32[8,64]{1,0:T(8,128)S(1)} %copy-done.4, ...), custom_call_target="tpu_custom_call" | custom-call | tf_op jit(solution)/shard_map/sweep_longitude/pallas_call | solution.py:134
  22.7 0.6 %collective-permute-start.2 = (f32[16,4,128]{2,1,0:T(4,128)S(1)}, f32[16,4,128]{2,1,0:T(4,128)S(1)}, u32[]{:S(2)}, u32[]{:S(2)}) collective-permute-start(f32[16,4,128]{2,1,0:T(4,128)S(1)} %get-tuple-element.14), channel_id=1, source_target_pairs={{0,1},{2,3},{1,0},{3,2},{4,5},{6,7},{5,4},{7,6},{8,9},{10,11},{9,8... | collective-permute-start | bytes 98312 | tf_op jit(solution)/shard_map/ppermute | solution.py:139
  23.4 0.7 %collective-permute-start.3 = (f32[16,4,128]{2,1,0:T(4,128)S(1)}, f32[16,4,128]{2,1,0:T(4,128)S(1)}, u32[]{:S(2)}, u32[]{:S(2)}) collective-permute-start(f32[16,4,128]{2,1,0:T(4,128)S(1)} %get-tuple-element.16), channel_id=1, source_target_pairs={{1,2},{2,1},{5,6},{6,5},{9,10},{10,9},{13,14},{14,13},{17,18},{18,... | collective-permute-start | bytes 98312 | tf_op jit(solution)/shard_map/ppermute | solution.py:139
  24.0 6.6 %all-to-all-done = f32[128,1,1280]{2,1,0:T(1,128)S(1)} async-done(((f32[128,1,1280]{2,1,0:T(1,128)}), f32[128,1,1280]{2,1,0:T(1,128)S(1)}, u32[]{:S(2)}, u32[]{:S(2)}) %all-to-all-start) | async-done | bytes 655392 | tf_op jit(solution)/shard_map/all_to_all | solution.py:289
  30.6 0.0 copy-done.3
  30.6 5.7 %owner_sums.1 = f32[4,6912]{1,0:T(4,128)} custom-call(f32[1280,128]{1,0:T(8,128)S(1)} %bitcast.2, s32[1,128,256]{2,1,0:T(8,128)S(1)} %copy-done.3), custom_call_target="tpu_custom_call" | custom-call | tf_op jit(solution)/shard_map/owner_sums/pallas_call | solution.py:276
  36.3 0.0 collective-permute-done.2.from_pair
  36.3 0.0 collective-permute-done.3.from_other
  36.3 0.0 copy-done.5
  36.3 1.2 %sweep_latitude.1 = f32[2,16,8,64]{3,2,1,0:T(8,128)} custom-call(f32[16,8,128]{2,1,0:T(8,128)S(1)} %get-tuple-element.13.swept, f32[16,8,64]{2,1,0:T(8,128)S(1)} %copy-done.2, s32[8,64]{1,0:T(8,128)S(1)} %copy-done.4, f32[16,8,64]{2,1,0:T(8,128)S(1)} %copy-done.5, f32[16,4,128]{2,1,0:T(4,128)S(1)} %collective-permute-done.2.from_pair, ...), custom_call_target="tpu_custom_call" | custom-call | tf_op jit(solution)/shard_map/sweep_latitude/pallas_call | solution.py:134
  (3 shorter events, 0.0 us)
Async XLA Ops:
  3.5 11.5 %copy-start = (f32[2,16,8,64]{3,2,1,0:T(8,128)S(1)}, f32[2,16,8,64]{3,2,1,0:T(8,128)}, u32[]{:S(2)}) copy-start(f32[2,16,8,64]{3,2,1,0:T(8,128)} %tracers.5) | copy-start | bytes 196612
  3.5 11.5 %copy-start.1 = (f32[16,8,64]{2,1,0:T(8,128)S(1)}, f32[16,8,64]{2,1,0:T(8,128)}, u32[]{:S(2)}) copy-start(f32[16,8,64]{2,1,0:T(8,128)} %u_face.5) | copy-start | bytes 98308
  3.5 11.5 %copy-start.4 = (s32[8,64]{1,0:T(8,128)S(1)}, s32[8,64]{1,0:T(8,128)}, u32[]{:S(2)}) copy-start(s32[8,64]{1,0:T(8,128)} %land_mask.7) | copy-start | bytes 6148
  3.5 27.1 %all-to-all-start = ((f32[128,1,1280]{2,1,0:T(1,128)}), f32[128,1,1280]{2,1,0:T(1,128)S(1)}, u32[]{:S(2)}, u32[]{:S(2)}) async-start(f32[128,1,1280]{2,1,0:T(1,128)} %bitcast.3), calls=%async_computation | async-start | bytes 1310720 | tf_op jit(solution)/shard_map/all_to_all | solution.py:289
  15.0 7.0 %copy-start.2 = (f32[16,8,64]{2,1,0:T(8,128)S(1)}, f32[16,8,64]{2,1,0:T(8,128)}, u32[]{:S(2)}) copy-start(f32[16,8,64]{2,1,0:T(8,128)} %v_face.5) | copy-start | bytes 98308
  15.3 4.0 %collective-permute-start = (f32[8,128]{1,0:T(8,128)S(1)}, f32[8,128]{1,0:T(8,128)S(1)}, u32[]{:S(2)}, u32[]{:S(2)}) collective-permute-start(f32[8,128]{1,0:T(8,128)S(1)} %get-tuple-element.11), channel_id=1, source_target_pairs={{0,4},{8,12},{16,20},{24,28},{32,36},{40,44},{48,52},{56,60},{64,6... | collective-permute-start | bytes 12296 | tf_op jit(solution)/shard_map/ppermute | solution.py:139
  16.5 14.1 %copy-start.3 = (s32[1,128,256]{2,1,0:T(8,128)S(1)}, s32[1,128,256]{2,1,0:T(8,128)}, u32[]{:S(2)}) copy-start(s32[1,128,256]{2,1,0:T(8,128)} %atm_cell.1) | copy-start | bytes 393220
  16.5 5.6 %collective-permute-start.1 = (f32[8,128]{1,0:T(8,128)S(1)}, f32[8,128]{1,0:T(8,128)S(1)}, u32[]{:S(2)}, u32[]{:S(2)}) collective-permute-start(f32[8,128]{1,0:T(8,128)S(1)} %get-tuple-element.12), channel_id=1, source_target_pairs={{4,8},{12,16},{20,24},{28,32},{36,40},{44,48},{52,56},{60,64},{68,... | collective-permute-start | bytes 12296 | tf_op jit(solution)/shard_map/ppermute | solution.py:139
  22.7 13.6 %collective-permute-start.2 = (f32[16,4,128]{2,1,0:T(4,128)S(1)}, f32[16,4,128]{2,1,0:T(4,128)S(1)}, u32[]{:S(2)}, u32[]{:S(2)}) collective-permute-start(f32[16,4,128]{2,1,0:T(4,128)S(1)} %get-tuple-element.14), channel_id=1, source_target_pairs={{0,1},{2,3},{1,0},{3,2},{4,5},{6,7},{5,4},{7,6},{8,9},{10,11},{9,8... | collective-permute-start | bytes 98312 | tf_op jit(solution)/shard_map/ppermute | solution.py:139
  23.4 13.0 %collective-permute-start.3 = (f32[16,4,128]{2,1,0:T(4,128)S(1)}, f32[16,4,128]{2,1,0:T(4,128)S(1)}, u32[]{:S(2)}, u32[]{:S(2)}) collective-permute-start(f32[16,4,128]{2,1,0:T(4,128)S(1)} %get-tuple-element.16), channel_id=1, source_target_pairs={{1,2},{2,1},{5,6},{6,5},{9,10},{10,9},{13,14},{14,13},{17,18},{18,... | collective-permute-start | bytes 98312 | tf_op jit(solution)/shard_map/ppermute | solution.py:139
  30.6 5.7 %copy-start.5 = (f32[16,8,64]{2,1,0:T(8,128)S(1)}, f32[16,8,64]{2,1,0:T(8,128)}, u32[]{:S(2)}) copy-start(f32[16,8,64]{2,1,0:T(8,128)} %thickness.1) | copy-start | bytes 98308

commit v5 on v4

--- a/solution.py
+++ b/solution.py
@@ -1,5 +1,3 @@
-import functools
-
 import jax
 import jax.numpy as jnp
 from jax import lax
@@ -8,8 +6,10 @@
 from jax.sharding import PartitionSpec as P
 
 A_DEV = 6912
-HI = 27
+PIECES = 3
 PER = 8
+F8 = jnp.float8_e4m3fn
+
 
 def lanes_of(shape):
     return lax.broadcasted_iota(jnp.int32, shape, len(shape) - 1)
@@ -128,10 +128,21 @@
         out[1, k] = total[:, 64:]
 
 VM = pl.BlockSpec(memory_space=pltpu.VMEM)
+ANY = pl.BlockSpec(memory_space=pl.ANY)
+
+
 def f32(*shape):
     return jax.ShapeDtypeStruct(shape, jnp.float32)
 def call(kernel, name, outs, args):
-    return pl.pallas_call(kernel, in_specs=[VM] * len(args), out_specs=[VM] * len(outs), out_shape=list(outs), compiler_params=pltpu.CompilerParams(vmem_limit_bytes=8 * 2**20), name=name)(*args)
+    return pl.pallas_call(
+        kernel,
+        in_specs=[VM] * len(args),
+        out_specs=[VM] * len(outs),
+        out_shape=list(outs),
+        compiler_params=pltpu.CompilerParams(vmem_limit_bytes=8 * 2**20),
+        name=name,
+    )(*args)
+
 
 def swap(x, axis, first):
     n = lax.axis_size(axis)
@@ -157,119 +168,168 @@
     return call(north_kernel, "sweep_latitude", [f32(2, 16, 8, 64)], args)[0]
 
 
+CHUNKS = 2
+
+
 def lane_take(table, lanes):
     return jnp.take_along_axis(table, lanes, axis=1, mode="promise_in_bounds")
-def gather_kernel(tracers, u_face, v_face, land_mask, counts, ocean_cell, weight, payload):
+
+
+def gather_kernel(
+    tracers, u_face, v_face, land_mask, counts, ocean_cell, weight, payload,
+    heat, east_in, north_in, mask, used_in, cells, shares, staged, small_sem, cell_sem, share_sem, out_sem,
+):
+    owners = 128 // CHUNKS
+    small = [
+        (tracers.at[:, 0], heat), (u_face.at[0], east_in), (v_face.at[0], north_in), (land_mask, mask), (counts, used_in),
+    ]
+    small = [pltpu.make_async_copy(src, dst, small_sem.at[i]) for i, (src, dst) in enumerate(small)]
+    for copy in small:
+        copy.start()
+    loads = []
+    for i in range(CHUNKS):
+        rows = pl.ds(i * owners, owners)
+        loads.append((
+            pltpu.make_async_copy(ocean_cell.at[0, rows], cells.at[rows], cell_sem.at[i]),
+            pltpu.make_async_copy(weight.at[0, rows], shares.at[rows], share_sem.at[i]),
+        ))
+        for copy in loads[-1]:
+            copy.start()
+    for copy in small:
+        copy.wait()
+
     def packed(x):
         return jnp.concatenate([x[0:4, :], x[4:8, :]], axis=1)
-    wet = packed(land_mask[...].astype(jnp.float32))
-    east = packed(u_face[0]); north = packed(v_face[0])
+
+    wet = packed(mask[...].astype(jnp.float32))
+    east = packed(east_in[...])
+    north = packed(north_in[...])
     speed = jnp.sqrt(east * east + north * north + 0.01) * wet
-    fields = [packed(tracers[0, 0]) * speed, packed(tracers[1, 0]) * speed, east * speed, north * speed, wet]
+    fields = [packed(heat[0]) * speed, packed(heat[1]) * speed, east * speed, north * speed, wet]
     tables = [[jnp.broadcast_to(f[q:q+1, :], (8, 128)) for q in range(4)] for f in fields]
-    used = jnp.broadcast_to(counts[...], (8, 128))
+    used = jnp.broadcast_to(used_in[...], (8, 128))
     sub = lax.broadcasted_iota(jnp.int32, (8, 128), 0)
     lane_ids = lax.broadcasted_iota(jnp.int32, (8, 128), 1)
-    def step(g, _):
-        o = pl.multiple_of(g * 8, 8)
-        count = lane_take(used, sub + o)
-        for h in range(2):
-            cell = ocean_cell[0, pl.ds(o, 8), h*128:(h+1)*128]
-            share = jnp.where(lane_ids + h*128 < count, weight[0, pl.ds(o, 8), h*128:(h+1)*128], 0.0)
-            lanes = (cell & 63) | ((cell >> 2) & 64)
-            odd = (cell & 64) != 0
-            upper = (cell & 128) != 0
-            for f in range(5):
-                a, b, c, d = [lane_take(t, lanes) for t in tables[f]]
-                val = jnp.where(upper, jnp.where(odd, d, c), jnp.where(odd, b, a))
-                payload[pl.ds(g * 80 + f*2+h, 8, stride=10), :] = val * share
-        return 0
-    lax.fori_loop(0, 16, step, 0, unroll=16)
+    stores = []
+    for i in range(CHUNKS):
+        for copy in loads[i]:
+            copy.wait()
+        for g in range(i * owners // 8, (i + 1) * owners // 8):
+            o = g * 8
+            count = lane_take(used, sub + o)
+            for h in range(2):
+                part = slice(h * 128, (h + 1) * 128)
+                cell = cells[o:o+8, part]
+                share = jnp.where(lane_ids + h * 128 < count, shares[o:o+8, part], 0.0)
+                lanes = (cell & 63) | ((cell >> 2) & 64)
+                odd = (cell & 64) != 0
+                upper = (cell & 128) != 0
+                for f in range(5):
+                    a, b, c, d = [lane_take(t, lanes) for t in tables[f]]
+                    val = jnp.where(upper, jnp.where(odd, d, c), jnp.where(odd, b, a))
+                    staged[pl.ds(g * 80 + f * 2 + h, 8, stride=10), :] = val * share
+        rows = pl.ds(i * owners * 10, owners * 10)
+        stores.append(pltpu.make_async_copy(staged.at[rows], payload.at[rows], out_sem.at[i]))
+        stores[-1].start()
+    for copy in stores:
+        copy.wait()
+
+
+def gather(tracers, u_face, v_face, land_mask, counts, ocean_cell, weight):
+    return pl.pallas_call(
+        gather_kernel,
+        in_specs=[ANY] * 7,
+        out_specs=ANY,
+        out_shape=f32(1280, 128),
+        scratch_shapes=[
+            pltpu.VMEM((2, 8, 64), jnp.float32),
+            pltpu.VMEM((8, 64), jnp.float32),
+            pltpu.VMEM((8, 64), jnp.float32),
+            pltpu.VMEM((8, 64), jnp.int32),
+            pltpu.VMEM((1, 128), jnp.int32),
+            pltpu.VMEM((128, 256), jnp.int32),
+            pltpu.VMEM((128, 256), jnp.float32),
+            pltpu.VMEM((1280, 128), jnp.float32),
+            pltpu.SemaphoreType.DMA((5,)),
+            pltpu.SemaphoreType.DMA((CHUNKS,)),
+            pltpu.SemaphoreType.DMA((CHUNKS,)),
+            pltpu.SemaphoreType.DMA((CHUNKS,)),
+        ],
+        name="weighted_slots",
+    )(tracers, u_face, v_face, land_mask, counts, ocean_cell, weight)
 
 
 def scatter_kernel(received, atm_cell, flux, fin):
     sub = lax.broadcasted_iota(jnp.int32, (16, 128), 0)
     def bf(x):
         return x.astype(jnp.float32).astype(jnp.bfloat16)
-    low_ids = [bf(sub + 16 * k) for k in range(16)]
-    high_ids = []
-    for k in range(17):
-        first = (16 * k) // HI
-        row = sub + 16 * k - first * HI
-        row = jnp.where(row >= HI, row - HI, row)
-        if k == 16:
-            row = jnp.where(sub < 14, row, -1)
-        high_ids.append(bf(row))
-    one, zero = jnp.bfloat16(1), jnp.bfloat16(0)
+    ids = [bf(sub + 16 * k) for k in range(16)]
+    zero8 = jnp.zeros((32, 128), F8)
+    one8 = jnp.ones((32, 128), F8)
     def spread(row):
         return jnp.broadcast_to(row, (16, 128)).astype(jnp.bfloat16)
+    peak = [jnp.zeros((8, 128), jnp.float32)] * 5
+    for g in range(16):
+        for f in range(5):
+            for h in range(2):
+                peak[f] = jnp.maximum(peak[f], jnp.abs(received[pl.ds(g * 80 + f*2+h, 8, stride=10), :]))
+    scale = []
+    back = []
+    for f in range(5):
+        top = jnp.maximum(jnp.max(jnp.max(peak[f], axis=0, keepdims=True), axis=1, keepdims=True), 1e-30)
+        scale.append(jnp.broadcast_to(224.0 / top, (8, 128)))
+        back.append(jnp.broadcast_to(top * (1.0 / 224.0), (8, 128)))
     def run(*accs):
-        accs = [accs[:17], accs[17:]]
+        n = len(accs) // 2
+        accs = [accs[:n], accs[n:]]
         for m in range(2):
             for a in accs[m]:
                 pltpu.matmul_pop(a)
         def chunk(cells, pieces, s, mxu, stage):
             low = [spread((c[s:s+1] & 255).astype(jnp.float32)) for c in cells]
-            rhs = jnp.concatenate([jnp.concatenate([jnp.where(lo == ids, one, zero) for lo in low], axis=1) for ids in low_ids], axis=0)
-            pltpu.matmul_push_rhs(rhs, stage, mxu, transpose=True)
             high = [spread((c[s:s+1] >> 8).astype(jnp.float32)) for c in cells]
-            tiles = {}
-            for k in range(17):
-                first = (16 * k) // HI
-                edge = (first + 1) * HI - 16 * k
-                for j in (first, first + 1):
-                    if j < 10 and j not in tiles:
-                        tiles[j] = [spread(p[s:s+1]) for p in pieces[j]]
+            cols = []
+            for h in range(2):
+                lo32 = jnp.concatenate([low[h], low[h]], axis=0)
+                rows = [jnp.where(lo32 == jnp.concatenate([ids[2*k], ids[2*k+1]], axis=0), one8, zero8) for k in range(8)]
+                cols.append(jnp.concatenate(rows, axis=0))
+            pltpu.matmul_push_rhs(jnp.concatenate(cols, axis=1), stage, mxu, transpose=True)
+            hit8 = [jnp.concatenate([x, x], axis=0) == jnp.concatenate([ids[0], ids[1]], axis=0) for x in high]
+            for j in range(5 * PIECES):
                 halves = []
                 for h in range(2):
-                    v = tiles[first][h]
-                    if edge < 16 and first + 1 < 10:
-                        v = jnp.where(sub < edge, v, tiles[first + 1][h])
-                    halves.append(jnp.where(high[h] == high_ids[k], v, zero))
-                pltpu.matmul_acc_lhs(accs[mxu][k], jnp.concatenate(halves, axis=1), load_staged_rhs=stage if k == 0 else None)
+                    v = jnp.broadcast_to(pieces[j][h][s:s+1], (32, 128)).astype(F8)
+                    halves.append(jnp.where(hit8[h], v, zero8))
+                pltpu.matmul_acc_lhs(accs[mxu][j], jnp.concatenate(halves, axis=1), load_staged_rhs=stage if j == 0 else None)
         def step(i, _):
             for k in range(PER):
                 g = i * PER + k
                 cells = [atm_cell[0, pl.ds(pl.multiple_of(g * 8, 8), 8), h*128:h*128+128] for h in range(2)]
                 pieces = []
                 for f in range(5):
-                    val = [received[pl.ds(g * 80 + f*2+h, 8, stride=10), :] for h in range(2)]
-                    top = [v.astype(jnp.bfloat16).astype(jnp.float32) for v in val]
-                    pieces += [top, [v - t for v, t in zip(val, top)]]
+                    rest = [received[pl.ds(g * 80 + f*2+h, 8, stride=10), :] * scale[f] for h in range(2)]
+                    for p in range(PIECES):
+                        part = [r.astype(F8).astype(jnp.float32) for r in rest]
+                        pieces.append(part)
+                        rest = [(r - t) * 16.0 for r, t in zip(rest, part)]
                 for s in range(8):
                     chunk(cells, pieces, s, s % 2, (s // 2) % 2)
             return 0
         lax.fori_loop(0, 16 // PER, step, 0)
-        for k in range(17):
-            total = pltpu.matmul_pop(accs[0][k]) + pltpu.matmul_pop(accs[1][k])
+        for f in range(5):
+            total = 0.0
+            for p in reversed(range(PIECES)):
+                total = total * (1.0 / 16.0) + (pltpu.matmul_pop(accs[0][f*PIECES+p]) + pltpu.matmul_pop(accs[1][f*PIECES+p]))
+            unit = jnp.concatenate([back[f]] * 4, axis=0)
             for half in range(2):
-                fin[half*272+k*16:half*272+k*16+16, :] = total[:, half*128:half*128+128]
-    pl.run_scoped(run, *([pltpu.ACC(0)((16, 256), jnp.float32)] * 17 + [pltpu.ACC(1)((16, 256), jnp.float32)] * 17))
+                fin[half*160+f*32:half*160+f*32+32, :] = total[:, half*128:half*128+128] * unit
+    pl.run_scoped(run, *([pltpu.ACC(0)((32, 256), jnp.float32)] * (5*PIECES) + [pltpu.ACC(1)((32, 256), jnp.float32)] * (5*PIECES)))
     for hi in range(27):
         for half in range(2):
-            b = half * 272 + hi
-            num = fin[pl.ds(b, 4, stride=54), :] + fin[pl.ds(b+27, 4, stride=54), :]
-            den = fin[b+216:b+217, :] + fin[b+243:b+244, :]
+            b = half * 160 + hi
+            num = fin[pl.ds(b, 4, stride=32), :]
+            den = fin[b+128:b+129, :]
             flux[:, hi*256+half*128:hi*256+half*128+128] = num / jnp.maximum(den, 0.2)
-
-
-def gather(tracers, u_face, v_face, land_mask, counts, ocean_cell, weight):
-    return pl.pallas_call(
-        gather_kernel,
-        grid=(1,),
-        in_specs=[
-            pl.BlockSpec((2, 1, 8, 64), lambda i: (0, 0, 0, 0)),
-            pl.BlockSpec((1, 8, 64), lambda i: (0, 0, 0)),
-            pl.BlockSpec((1, 8, 64), lambda i: (0, 0, 0)),
-            pl.BlockSpec((8, 64), lambda i: (0, 0)),
-            pl.BlockSpec((1, 128), lambda i: (0, 0)),
-            pl.BlockSpec((1, 128, 256), lambda i: (0, 0, 0)),
-            pl.BlockSpec((1, 128, 256), lambda i: (0, 0, 0)),
-        ],
-        out_specs=pl.BlockSpec((1280, 128), lambda i: (0, 0)),
-        out_shape=f32(1280, 128),
-        name="weighted_slots",
-    )(tracers, u_face, v_face, land_mask, counts, ocean_cell, weight)
 
 
 def scatter(received, atm_cell):
@@ -278,7 +338,7 @@
         in_specs=[VM] * 2,
         out_specs=VM,
         out_shape=f32(4, A_DEV),
-        scratch_shapes=[pltpu.VMEM((544, 128), jnp.float32)],
+        scratch_shapes=[pltpu.VMEM((320, 128), jnp.float32)],
         compiler_params=pltpu.CompilerParams(vmem_limit_bytes=16 * 2**20),
         name="owner_sums",
     )(received, atm_cell)

time: 37.7 us -> 37.1 us (0.984)
  Pallas kernels: 10.7 us -> 10 us
    pallas_call x1, Pallas kernels: 5.71 us -> 5.16 us  [scatter(): pl.pallas_call(scatter_kernel, in_specs=[VM] * 2, out_specs=VM, out_shape...]
  transfers between devices with their start and end apart: 5 -> 5, of which waited for: 2 -> 2; matrix products, arithmetic and copies ran while one was open for 0% -> 0% of each run, Pallas kernels for 18% -> 17%
where the time goes in v5:
time: 37.1 us; the launch traced here: 36.8 us
  starting transfers between devices  16.8 us (45%)
  Pallas kernels  10 us (27%)
  waiting for transfers between devices  9.27 us (25%)
  between operations  0.74 us (2%)
    all_to_all x1, starting transfers between devices, on_device(): lax.all_to_all(payload.reshape(128, 1, 1280), ('gx', 'gy'), split_axis=0,...  11.5 us
    all_to_all x1, waiting for transfers between devices, on_device(): lax.all_to_all(payload.reshape(128, 1, 1280), ('gx', 'gy'), split_axis=0,...  6.58 us
    ppermute x4, starting transfers between devices, swap(): return lax.ppermute(x, axis, pairs + [(j, i) for i, j in pairs])  5.28 us
    pallas_call x1, Pallas kernels, scatter(): pl.pallas_call(scatter_kernel, in_specs=[VM] * 2, out_specs=VM, out_shape...  5.16 us
    pallas_call x1, Pallas kernels, gather(): pl.pallas_call(gather_kernel, in_specs=[ANY] * 7, out_specs=ANY, out_shap...  2.72 us
    ppermute x4, waiting for transfers between devices, swap(): return lax.ppermute(x, axis, pairs + [(j, i) for i, j in pairs])  2.69 us
    pallas_call x3, Pallas kernels, call(): pl.pallas_call(kernel, in_specs=[VM] * len(args), out_specs=[VM] * len(ou...  2.13 us
  transfers between devices with their start and end apart: 5, of which 2 were waited for; matrix products, arithmetic and copies ran while one was open for 0% of the time, Pallas kernels for 17%

profile of v5, /device:TPU:1, one launch (start us, length us, event | category | flops | bytes accessed | tf_op | source)
XLA Modules:
  0.0 36.8 jit_solution(1229751638267682491)
XLA Ops:
  0.6 2.7 %weighted_slots.1 = f32[1280,128]{1,0:T(8,128)} custom-call(f32[2,16,8,64]{3,2,1,0:T(8,128)} %tracers.5, f32[16,8,64]{2,1,0:T(8,128)} %u_face.5, f32[16,8,64]{2,1,0:T(8,128)} %v_face.5, s32[8,64]{1,0:T(8,128)} %land_mask.7, s32[1,128]{1,0:T(1,128)} %counts.1, s32[1,128,256]{2,1,0:T(8,128)} %ocean_cell.1, f32[1,128,256]{2,1,0:T(8,128)} %weight.1), custom_call_target="tpu_custom_call" | custom-call | tf_op jit(solution)/shard_map/weighted_slots/pallas_call | solution.py:239
  3.4 0.0 copy-start
  3.4 0.0 copy-start.1
  3.4 0.0 copy-start.4
  3.4 11.5 %all-to-all-start = ((f32[128,1,1280]{2,1,0:T(1,128)}), f32[128,1,1280]{2,1,0:T(1,128)S(1)}, u32[]{:S(2)}, u32[]{:S(2)}) async-start(f32[128,1,1280]{2,1,0:T(1,128)} %bitcast.3), calls=%async_computation | async-start | bytes 1310720 | tf_op jit(solution)/shard_map/all_to_all | solution.py:349
  14.9 0.0 copy-done
  14.9 0.0 copy-done.1
  14.9 0.0 copy-done.4
  14.9 0.0 copy-start.2
  14.9 0.3 column_strips.1
  15.2 1.1 %collective-permute-start = (f32[8,128]{1,0:T(8,128)S(1)}, f32[8,128]{1,0:T(8,128)S(1)}, u32[]{:S(2)}, u32[]{:S(2)}) collective-permute-start(f32[8,128]{1,0:T(8,128)S(1)} %get-tuple-element.11), channel_id=1, source_target_pairs={{0,4},{8,12},{16,20},{24,28},{32,36},{40,44},{48,52},{56,60},{64,6... | collective-permute-start | bytes 12296 | tf_op jit(solution)/shard_map/ppermute | solution.py:150
  16.3 2.9 %collective-permute-start.1 = (f32[8,128]{1,0:T(8,128)S(1)}, f32[8,128]{1,0:T(8,128)S(1)}, u32[]{:S(2)}, u32[]{:S(2)}) collective-permute-start(f32[8,128]{1,0:T(8,128)S(1)} %get-tuple-element.12), channel_id=1, source_target_pairs={{4,8},{12,16},{20,24},{28,32},{36,40},{44,48},{52,56},{60,64},{68,... | collective-permute-start | bytes 12296 | tf_op jit(solution)/shard_map/ppermute | solution.py:150
  19.2 0.0 collective-permute-done.from_near
  19.2 2.7 %collective-permute-done.1.from_far = f32[8,128]{1,0:T(8,128)S(1)} collective-permute-done((f32[8,128]{1,0:T(8,128)S(1)}, f32[8,128]{1,0:T(8,128)S(1)}, u32[]{:S(2)}, u32[]{:S(2)}) %collective-permute-start.1) | collective-permute-done | bytes 4128 | tf_op jit(solution)/shard_map/ppermute | solution.py:150
  21.9 0.0 copy-done.2
  21.9 0.7 %sweep_longitude.1 = (f32[16,8,128]{2,1,0:T(8,128)S(1)}, f32[16,4,128]{2,1,0:T(4,128)S(1)}, f32[16,4,128]{2,1,0:T(4,128)S(1)}) custom-call(f32[2,16,8,64]{3,2,1,0:T(8,128)S(1)} %copy-done, f32[16,8,64]{2,1,0:T(8,128)S(1)} %copy-done.1, f32[16,8,64]{2,1,0:T(8,128)S(1)} %copy-done.2, s32[8,64]{1,0:T(8,128)S(1)} %copy-done.4, ...), custom_call_target="tpu_custom_call" | custom-call | tf_op jit(solution)/shard_map/sweep_longitude/pallas_call | solution.py:137
  22.6 0.6 %collective-permute-start.2 = (f32[16,4,128]{2,1,0:T(4,128)S(1)}, f32[16,4,128]{2,1,0:T(4,128)S(1)}, u32[]{:S(2)}, u32[]{:S(2)}) collective-permute-start(f32[16,4,128]{2,1,0:T(4,128)S(1)} %get-tuple-element.14), channel_id=1, source_target_pairs={{0,1},{2,3},{1,0},{3,2},{4,5},{6,7},{5,4},{7,6},{8,9},{10,11},{9,8... | collective-permute-start | bytes 98312 | tf_op jit(solution)/shard_map/ppermute | solution.py:150
  23.3 0.7 %collective-permute-start.3 = (f32[16,4,128]{2,1,0:T(4,128)S(1)}, f32[16,4,128]{2,1,0:T(4,128)S(1)}, u32[]{:S(2)}, u32[]{:S(2)}) collective-permute-start(f32[16,4,128]{2,1,0:T(4,128)S(1)} %get-tuple-element.16), channel_id=1, source_target_pairs={{1,2},{2,1},{5,6},{6,5},{9,10},{10,9},{13,14},{14,13},{17,18},{18,... | collective-permute-start | bytes 98312 | tf_op jit(solution)/shard_map/ppermute | solution.py:150
  23.9 6.6 %all-to-all-done = f32[128,1,1280]{2,1,0:T(1,128)S(1)} async-done(((f32[128,1,1280]{2,1,0:T(1,128)}), f32[128,1,1280]{2,1,0:T(1,128)S(1)}, u32[]{:S(2)}, u32[]{:S(2)}) %all-to-all-start) | async-done | bytes 655392 | tf_op jit(solution)/shard_map/all_to_all | solution.py:349
  30.5 0.0 copy-done.3
  30.5 5.2 %owner_sums.1 = f32[4,6912]{1,0:T(4,128)} custom-call(f32[1280,128]{1,0:T(8,128)S(1)} %bitcast.2, s32[1,128,256]{2,1,0:T(8,128)S(1)} %copy-done.3), custom_call_target="tpu_custom_call" | custom-call | tf_op jit(solution)/shard_map/owner_sums/pallas_call | solution.py:336
  35.6 0.0 collective-permute-done.2.from_pair
  35.7 0.0 collective-permute-done.3.from_other
  35.7 1.2 %sweep_latitude.1 = f32[2,16,8,64]{3,2,1,0:T(8,128)} custom-call(f32[16,8,128]{2,1,0:T(8,128)S(1)} %get-tuple-element.13.swept, f32[16,8,64]{2,1,0:T(8,128)S(1)} %copy-done.2, s32[8,64]{1,0:T(8,128)S(1)} %copy-done.4, f32[16,8,64]{2,1,0:T(8,128)S(1)} %copy-done.5, f32[16,4,128]{2,1,0:T(4,128)S(1)} %collective-permute-done.2.from_pair, ...), custom_call_target="tpu_custom_call" | custom-call | tf_op jit(solution)/shard_map/sweep_latitude/pallas_call | solution.py:137
  (3 shorter events, 0.0 us)
Async XLA Ops:
  3.4 11.5 %copy-start = (f32[2,16,8,64]{3,2,1,0:T(8,128)S(1)}, f32[2,16,8,64]{3,2,1,0:T(8,128)}, u32[]{:S(2)}) copy-start(f32[2,16,8,64]{3,2,1,0:T(8,128)} %tracers.5) | copy-start | bytes 196612
  3.4 11.5 %copy-start.1 = (f32[16,8,64]{2,1,0:T(8,128)S(1)}, f32[16,8,64]{2,1,0:T(8,128)}, u32[]{:S(2)}) copy-start(f32[16,8,64]{2,1,0:T(8,128)} %u_face.5) | copy-start | bytes 98308
  3.4 11.5 %copy-start.4 = (s32[8,64]{1,0:T(8,128)S(1)}, s32[8,64]{1,0:T(8,128)}, u32[]{:S(2)}) copy-start(s32[8,64]{1,0:T(8,128)} %land_mask.7) | copy-start | bytes 6148
  3.4 27.1 %all-to-all-start = ((f32[128,1,1280]{2,1,0:T(1,128)}), f32[128,1,1280]{2,1,0:T(1,128)S(1)}, u32[]{:S(2)}, u32[]{:S(2)}) async-start(f32[128,1,1280]{2,1,0:T(1,128)} %bitcast.3), calls=%async_computation | async-start | bytes 1310720 | tf_op jit(solution)/shard_map/all_to_all | solution.py:349
  14.9 7.0 %copy-start.2 = (f32[16,8,64]{2,1,0:T(8,128)S(1)}, f32[16,8,64]{2,1,0:T(8,128)}, u32[]{:S(2)}) copy-start(f32[16,8,64]{2,1,0:T(8,128)} %v_face.5) | copy-start | bytes 98308
  15.2 4.0 %collective-permute-start = (f32[8,128]{1,0:T(8,128)S(1)}, f32[8,128]{1,0:T(8,128)S(1)}, u32[]{:S(2)}, u32[]{:S(2)}) collective-permute-start(f32[8,128]{1,0:T(8,128)S(1)} %get-tuple-element.11), channel_id=1, source_target_pairs={{0,4},{8,12},{16,20},{24,28},{32,36},{40,44},{48,52},{56,60},{64,6... | collective-permute-start | bytes 12296 | tf_op jit(solution)/shard_map/ppermute | solution.py:150
  16.3 14.1 %copy-start.3 = (s32[1,128,256]{2,1,0:T(8,128)S(1)}, s32[1,128,256]{2,1,0:T(8,128)}, u32[]{:S(2)}) copy-start(s32[1,128,256]{2,1,0:T(8,128)} %atm_cell.1) | copy-start | bytes 393220
  16.3 5.6 %collective-permute-start.1 = (f32[8,128]{1,0:T(8,128)S(1)}, f32[8,128]{1,0:T(8,128)S(1)}, u32[]{:S(2)}, u32[]{:S(2)}) collective-permute-start(f32[8,128]{1,0:T(8,128)S(1)} %get-tuple-element.12), channel_id=1, source_target_pairs={{4,8},{12,16},{20,24},{28,32},{36,40},{44,48},{52,56},{60,64},{68,... | collective-permute-start | bytes 12296 | tf_op jit(solution)/shard_map/ppermute | solution.py:150
  22.6 13.0 %collective-permute-start.2 = (f32[16,4,128]{2,1,0:T(4,128)S(1)}, f32[16,4,128]{2,1,0:T(4,128)S(1)}, u32[]{:S(2)}, u32[]{:S(2)}) collective-permute-start(f32[16,4,128]{2,1,0:T(4,128)S(1)} %get-tuple-element.14), channel_id=1, source_target_pairs={{0,1},{2,3},{1,0},{3,2},{4,5},{6,7},{5,4},{7,6},{8,9},{10,11},{9,8... | collective-permute-start | bytes 98312 | tf_op jit(solution)/shard_map/ppermute | solution.py:150
  23.3 12.4 %collective-permute-start.3 = (f32[16,4,128]{2,1,0:T(4,128)S(1)}, f32[16,4,128]{2,1,0:T(4,128)S(1)}, u32[]{:S(2)}, u32[]{:S(2)}) collective-permute-start(f32[16,4,128]{2,1,0:T(4,128)S(1)} %get-tuple-element.16), channel_id=1, source_target_pairs={{1,2},{2,1},{5,6},{6,5},{9,10},{10,9},{13,14},{14,13},{17,18},{18,... | collective-permute-start | bytes 98312 | tf_op jit(solution)/shard_map/ppermute | solution.py:150
  30.5 5.2 %copy-start.5 = (f32[16,8,64]{2,1,0:T(8,128)S(1)}, f32[16,8,64]{2,1,0:T(8,128)}, u32[]{:S(2)}) copy-start(f32[16,8,64]{2,1,0:T(8,128)} %thickness.1) | copy-start | bytes 98308
